TPU v7x, 128 devices: a whole 4x4x4 slice. The times are simulated.
128 devices in a mesh: dp: 8 (over x, core), fsdp: 16 (over y, z).
Axes of the slice: x: 4, y: 4, z: 4, core: 2. Of those that a mesh axis runs over, the one named last changes fastest.
Arguments:
- queries: bfloat16 [24576, 4096], P(('dp', 'fsdp')), may hold values from -6 to 6
- passages: bfloat16 [24576, 4096], P(('dp', 'fsdp')), may hold values from -6 to 6
- head_weight: bfloat16 [4096, 2048], P('fsdp'), may hold values from -0.09375 to 0.09375
- send_lists: int32 [8, 16, 8, 48], P('dp', 'fsdp'), may hold values from 0 to 191
- neg_slots: int32 [24576, 16], P(('dp', 'fsdp')), may hold values from 0 to 383
Outputs:
- query_grads: bfloat16 [24576, 4096], P(('dp', 'fsdp'))
- passage_grads: bfloat16 [24576, 4096], P(('dp', 'fsdp'))
- head_grads: float32 [4096, 2048], P('fsdp', 'dp')
All inputs are finite; a program needn't handle non-finite values.
Results may differ from a plain program's by a relative error of at most 0.025.
Values may be sent and summed in bfloat16 or wider, within the bound.
No kernel may reach another device: no remote copies, remote signals or barrier semaphores. Data moves between devices by JAX's collectives and lax.ppermute only.
A program may use at most 128 MiB of HBM per device.

v0:
```python
import jax
import jax.numpy as jnp
from jax import lax
from jax.experimental import pallas as pl
from jax.experimental.pallas import tpu as pltpu
from jax.sharding import Mesh, PartitionSpec as P

EPSILON = 1e-06
BLOCK = 256
RING = 4
SWAP = [(0, 1), (1, 0)]
BF16 = jnp.bfloat16
F32 = jnp.float32


def shift(value, place, step):
    pairs = []
    for c in range(2):
        for y in range(RING):
            for z in range(RING):
                to_y, to_z = y, z
                if (place == 1) == (c == 0):
                    to_y = (y + step) % RING
                else:
                    to_z = (z + step) % RING
                pairs.append((c * 16 + y * 4 + z, c * 16 + to_y * 4 + to_z))
    return lax.ppermute(value, ("c", "y", "z"), pairs)


def swap(value):
    return lax.ppermute(value, "c", SWAP)


def block_at(core, d1, d2):
    y, z = lax.axis_index("y"), lax.axis_index("z")
    far_y = jnp.where(core == 0, d1, d2)
    far_z = jnp.where(core == 0, d2, d1)
    return ((y + far_y) % RING) * RING + (z + far_z) % RING


def together(*values):
    return lax.optimization_barrier(values)


def turn_kernel(*refs):
    parts = 4
    x_refs, turned_ref, held, turned, loaded, stored = refs[:4], *refs[4:]
    rows, depth = x_refs[0].shape
    size = depth // parts
    loads, stores = [], []
    for i in range(parts):
        at = pl.ds(i * size, size)
        loads.append(
            [
                pltpu.make_async_copy(ref.at[:, at], held.at[pl.ds(j * rows, rows), at], loaded.at[i, j])
                for j, ref in enumerate(x_refs)
            ]
        )
        stores.append(pltpu.make_async_copy(turned.at[at, :], turned_ref.at[at, :], stored.at[i]))
    for load in loads:
        start(load)
    for i in range(parts):
        wait(loads[i])
        for k in range(size // BLOCK):
            at = pl.ds(i * size + k * BLOCK, BLOCK)
            turned[at, :] = held[:, at].T
        stores[i].start()
    wait(stores)


def turn(*states):
    rows, depth = states[0].shape
    whole = rows * len(states)
    anywhere = pl.BlockSpec(memory_space=pl.ANY)
    return pl.pallas_call(
        turn_kernel,
        in_specs=[anywhere] * len(states),
        out_specs=anywhere,
        out_shape=pltpu.HBM((depth, whole), BF16),
        scratch_shapes=[
            pltpu.VMEM((whole, depth), BF16),
            pltpu.VMEM((depth, whole), BF16),
            pltpu.SemaphoreType.DMA((4, len(states))),
            pltpu.SemaphoreType.DMA((4,)),
        ],
        compiler_params=pltpu.CompilerParams(vmem_limit_bytes=20 * 1024 * 1024),
        cost_estimate=pl.CostEstimate(flops=1, transcendentals=0, bytes_accessed=1),
        name="turn",
    )(*keep_far(*states[:2]), *states[2:])


def copies_of(pairs, sems):
    return [pltpu.make_async_copy(*pair, sems.at[i]) for i, pair in enumerate(pairs)]


def start(copies):
    for copy in copies:
        copy.start()


def wait(copies):
    for copy in copies:
        copy.wait()


def head_copies(at_ref, held, head_ref, side, blocks, sems):
    col = pl.multiple_of(at_ref[1, side] * 1024, 1024)
    pairs = []
    for k in blocks:
        row = pl.multiple_of(at_ref[0, 16 * side + k] * BLOCK, BLOCK)
        pairs.append(
            (
                held.at[side, pl.ds((k - blocks[0]) * BLOCK, BLOCK), :],
                head_ref.at[pl.ds(row, BLOCK), pl.ds(col, 1024)],
            )
        )
    return copies_of(pairs, sems)


def piece_copies(pieces, held, side, sems):
    row, pairs = 0, []
    for piece in pieces:
        pairs.append((piece, held.at[side, pl.ds(row, piece.shape[0]), :]))
        row += piece.shape[0]
    return copies_of(pairs, sems)


def column_copies(at_ref, side, blocks, sources, states, sems):
    pairs = []
    for i, k in enumerate(blocks):
        col, row = pl.multiple_of(at_ref[0, 16 * side + k] * BLOCK, BLOCK), 0
        for ref in sources:
            to = states.at[side, pl.ds(row, ref.shape[0]), pl.ds(i * BLOCK, BLOCK)]
            pairs.append((ref.at[:, pl.ds(col, BLOCK)], to))
            row += ref.shape[0]
    return copies_of(pairs, sems)


def strips(at_ref, side, body, unroll=1):
    def one(n, _):
        at_col = pl.multiple_of(n * BLOCK, BLOCK)
        body(pl.ds(at_col, BLOCK), pl.ds(pl.multiple_of(at_ref[1, side] * 1024 + at_col, BLOCK), BLOCK))
        return 0

    lax.fori_loop(0, 1024 // BLOCK, one, 0, unroll=unroll)


def project_early_kernel(count, at_ref, *refs):
    x_refs, pieces = refs[:2], refs[2 : 2 + 2 * count]
    head_ref, part_out, states, held, part_ref, fetched, loaded, stored, parted = refs[2 + 2 * count :]
    blocks = list(range(held.shape[1] // BLOCK))
    loads = [
        column_copies(at_ref, i, blocks, x_refs, states, fetched.at[i])
        + piece_copies(pieces[i * count : (i + 1) * count], held, i, loaded.at[i])
        for i in range(2)
    ]
    stores = [head_copies(at_ref, held, head_ref, i, blocks, stored.at[i]) for i in range(2)]
    outs = []
    start(loads[0])
    for side in range(2):
        wait(loads[side])
        start(loads[1] if side == 0 else stores[0] + stores[1])

        def multiply(near_at, whole_at, side=side):
            part_ref[:, whole_at] = jnp.dot(
                states[side], held[side, :, near_at], preferred_element_type=F32
            ).astype(BF16)

        strips(at_ref, side, multiply)
        whole = pl.ds(pl.multiple_of(at_ref[1, side] * 1024, 1024), 1024)
        outs.append(pltpu.make_async_copy(part_ref.at[:, whole], part_out.at[:, whole], parted.at[side]))
        start(outs[side:])
    wait(outs + stores[0] + stores[1])


def project_early(at, xs, pieces):
    count, depth = len(pieces) // 2, sum(piece.shape[0] for piece in pieces) // 2
    rows = sum(x.shape[0] for x in xs)
    anywhere = pl.BlockSpec(memory_space=pl.ANY)
    return pl.pallas_call(
        lambda *refs: project_early_kernel(count, *refs),
        in_specs=[pl.BlockSpec(memory_space=pltpu.SMEM)] + [anywhere] * (2 + 2 * count),
        out_specs=[anywhere] * 2,
        out_shape=[pltpu.HBM((4096, 2048), BF16), pltpu.HBM((rows, 2048), BF16)],
        scratch_shapes=[
            pltpu.VMEM((2, rows, depth), BF16),
            pltpu.VMEM((2, depth, 1024), BF16),
            pltpu.VMEM((rows, 2048), BF16),
            pltpu.SemaphoreType.DMA((2, 2 * depth // BLOCK)),
            pltpu.SemaphoreType.DMA((2, count)),
            pltpu.SemaphoreType.DMA((2, depth // BLOCK)),
            pltpu.SemaphoreType.DMA((2,)),
        ],
        compiler_params=pltpu.CompilerParams(vmem_limit_bytes=24 * 1024 * 1024),
        name="project_early",
    )(at, *keep_far(*xs, *pieces))


def project_middle_kernel(count, early, at_ref, *refs):
    x_refs, pieces = refs[:3], refs[3 : 3 + 2 * count]
    part_in, _, head_ref, part_out = refs[3 + 2 * count : 7 + 2 * count]
    own_states, far_states, held, part_ref, fetched, loaded, stored, parted = refs[7 + 2 * count :]
    rows, depth = far_states.shape[1], held.shape[1]
    blocks = list(range(depth // BLOCK))
    late = early * BLOCK
    base = copies_of([(part_in, part_ref.at[pl.ds(0, rows), :])], parted.at[2])
    loads = [
        column_copies(at_ref, i, blocks, x_refs[2:], far_states, fetched.at[2 * i])
        + piece_copies(pieces[i * count : (i + 1) * count], held, i, loaded.at[i])
        + column_copies(at_ref, i, blocks[early:], x_refs[:2], own_states, fetched.at[2 * i + 1])
        for i in range(2)
    ]
    stores = [head_copies(at_ref, held, head_ref, i, blocks, stored.at[i])[early:] for i in range(2)]
    outs = []
    start(loads[0] + base)
    for side in range(2):
        wait(loads[side])
        start(loads[1] if side == 0 else stores[0] + stores[1])
        if side == 0:
            wait(base)

        def multiply(near_at, whole_at, side=side):
            own_at = pl.ds(0, rows)
            part_ref[own_at, whole_at] = (
                part_ref[own_at, whole_at].astype(F32)
                + jnp.dot(
                    own_states[side],
                    held[side, pl.ds(late, depth - late), near_at],
                    preferred_element_type=F32,
                )
            ).astype(BF16)
            part_ref[pl.ds(rows, rows), whole_at] = jnp.dot(
                far_states[side], held[side, :, near_at], preferred_element_type=F32
            ).astype(BF16)

        strips(at_ref, side, multiply)
        whole = pl.ds(pl.multiple_of(at_ref[1, side] * 1024, 1024), 1024)
        outs.append(
            pltpu.make_async_copy(part_ref.at[:, whole], part_out.at[:, whole], parted.at[side, 0])
        )
        start(outs[side:])
    wait(outs + stores[0] + stores[1])


def project_middle(at, early, xs, pieces, part, head):
    count, depth = len(pieces) // 2, sum(piece.shape[0] for piece in pieces) // 2
    rows = xs[2].shape[0]
    anywhere = pl.BlockSpec(memory_space=pl.ANY)
    ins = [anywhere] * (5 + 2 * count)
    return pl.pallas_call(
        lambda *refs: project_middle_kernel(count, early, *refs),
        in_specs=[pl.BlockSpec(memory_space=pltpu.SMEM)] + ins,
        out_specs=[anywhere] * 2,
        out_shape=[pltpu.HBM((4096, 2048), BF16), pltpu.HBM((2 * rows, 2048), BF16)],
        scratch_shapes=[
            pltpu.VMEM((2, rows, depth - early * BLOCK), BF16),
            pltpu.VMEM((2, rows, depth), BF16),
            pltpu.VMEM((2, depth, 1024), BF16),
            pltpu.VMEM((2 * rows, 2048), BF16),
            pltpu.SemaphoreType.DMA((4, 16)),
            pltpu.SemaphoreType.DMA((2, count)),
            pltpu.SemaphoreType.DMA((2, depth // BLOCK)),
            pltpu.SemaphoreType.DMA((3, 1)),
        ],
        input_output_aliases={len(ins): 0},
        compiler_params=pltpu.CompilerParams(vmem_limit_bytes=36 * 1024 * 1024),
        name="project_middle",
    )(at, *keep_far(*xs, *pieces, part, head))


def project_last_kernel(count, at_ref, *refs):
    x_refs, pieces = refs[:3], refs[3 : 3 + 2 * count]
    part_in, counts_ref, _, head_ref, emb_out, inverse_ref, mixing_ref, first_ref, grad_ref = refs[
        3 + 2 * count : 12 + 2 * count
    ]
    states, held, part_ref, pre_ref, emb_ref, parted, fetched, loaded, stored, sent = refs[12 + 2 * count :]
    late = held.shape[1] // BLOCK
    blocks = list(range(16 - late, 16))
    loads, stores = [], []
    for side in range(2):
        copies = column_copies(at_ref, side, blocks, x_refs, states, fetched.at[side])
        copies += piece_copies(pieces[side * count : (side + 1) * count], held, side, loaded.at[side])
        loads.append(copies)
        stores.append(head_copies(at_ref, held, head_ref, side, blocks, stored.at[side]))
    halves = [pl.ds(pl.multiple_of(at_ref[1, side] * 1024, 1024), 1024) for side in range(2)]
    base = copies_of([(part_in.at[:, at], part_ref.at[:, at]) for at in halves], parted)
    start(loads[0] + base[:1] + loads[1] + base[1:])
    inverse_ref[...] = jnp.zeros(inverse_ref.shape, F32)
    for side in range(2):
        wait(loads[side] + base[side : side + 1])
        if side == 1:
            start(stores[0] + stores[1])

        def multiply(near_at, whole_at, side=side):
            values = part_ref[:, whole_at].astype(F32) + jnp.dot(
                states[side], held[side, :, near_at], preferred_element_type=F32
            )
            pre_ref[:, whole_at] = values
            squares = values * values
            inverse_ref[...] += squares[:, :128] + squares[:, 128:]

        strips(at_ref, side, multiply, 4)
    normalize(pre_ref, emb_ref, inverse_ref)
    sending = copies_of([(emb_ref, emb_out)], sent)
    start(sending)
    contrast(counts_ref, emb_ref, mixing_ref, first_ref, grad_ref)
    wait(sending + stores[0] + stores[1])


def project_last(at, xs, pieces, part, counts, head):
    count, depth = len(pieces) // 2, sum(piece.shape[0] for piece in pieces) // 2
    rows = sum(x.shape[0] for x in xs)
    half = rows // 4
    anywhere = pl.BlockSpec(memory_space=pl.ANY)
    ins = [anywhere] * (4 + 2 * count) + vmem(1) + [anywhere]
    return pl.pallas_call(
        lambda *refs: project_last_kernel(count, *refs),
        in_specs=[pl.BlockSpec(memory_space=pltpu.SMEM)] + ins,
        out_specs=[anywhere] * 2 + vmem(4),
        out_shape=[
            pltpu.HBM((4096, 2048), BF16),
            pltpu.HBM((rows, 2048), BF16),
            pltpu.HBM((rows, 128), F32),
            pltpu.HBM((half, 2 * half), BF16),
            pltpu.HBM((half, 128), F32),
            pltpu.HBM((2 * half, 2048), BF16),
        ],
        scratch_shapes=[
            pltpu.VMEM((2, rows, depth), BF16),
            pltpu.VMEM((2, depth, 1024), BF16),
            pltpu.VMEM((rows, 2048), BF16),
            pltpu.VMEM((rows, 2048), F32),
            pltpu.VMEM((rows, 2048), BF16),
            pltpu.SemaphoreType.DMA((2,)),
            pltpu.SemaphoreType.DMA((2, 3 * depth // BLOCK)),
            pltpu.SemaphoreType.DMA((2, count)),
            pltpu.SemaphoreType.DMA((2, depth // BLOCK)),
            pltpu.SemaphoreType.DMA((1,)),
        ],
        input_output_aliases={len(ins): 0},
        compiler_params=pltpu.CompilerParams(vmem_limit_bytes=30 * 1024 * 1024),
        name="project_last",
    )(at, *keep_far(*xs, *pieces, part), counts, *keep_far(head))


def normalize(pre_ref, emb_ref, inverse_ref):
    chunk = 128
    width = pre_ref.shape[1]

    def some(i, _):
        at = pl.ds(pl.multiple_of(i * chunk, chunk), chunk)
        mean = jnp.sum(inverse_ref[at, :], axis=-1, keepdims=True) * (1.0 / width)
        inverse = jnp.broadcast_to(lax.rsqrt(mean + EPSILON), (chunk, 128))
        inverse_ref[at, :] = inverse
        emb_ref[at, :] = (pre_ref[at, :] * inverse[:, :1]).astype(BF16)
        return 0

    lax.fori_loop(0, pre_ref.shape[0] // chunk, some, 0)


def contrast(counts_ref, emb_ref, mixing_ref, first_ref, grad_ref):
    rows = counts_ref.shape[0]
    scale = 16.0 / emb_ref.shape[1]
    query = emb_ref[pl.ds(0, rows), :]
    passage = emb_ref[pl.ds(rows, rows), :]
    fetched = emb_ref[pl.ds(2 * rows, 2 * rows), :]
    positive = (
        jnp.sum(query.astype(F32) * passage.astype(F32), axis=1, keepdims=True) * scale
    )
    table = dot(query, fetched, ((1,), (1,))) * scale
    counts = counts_ref[...]
    top = jnp.maximum(
        positive, jnp.max(jnp.where(counts > 0, table, -1e30), axis=1, keepdims=True)
    )
    raised = jnp.where(counts > 0, jnp.exp(jnp.where(counts > 0, table - top, 0.0)), 0.0)
    raised_positive = jnp.exp(positive - top)
    whole = raised_positive + jnp.sum(raised * counts, axis=1, keepdims=True)
    first = (raised_positive / whole - 1.0).astype(BF16).astype(F32)
    mixing = ((raised / whole).astype(BF16).astype(F32) * counts).astype(BF16)
    first_ref[...] = jnp.broadcast_to(first, (rows, 128))
    mixing_ref[...] = mixing
    grad_ref[...] = dot(mixing, query, ((0,), (0,))).astype(BF16)


def vmem(count):
    return [pl.BlockSpec(memory_space=pltpu.VMEM)] * count


def near(shape, dtype):
    return pltpu.VMEM(shape, dtype)


def keep_near(*values):
    return [pltpu.with_memory_space_constraint(value, pltpu.VMEM) for value in values]


def keep_far(*values):
    return [pltpu.with_memory_space_constraint(value, pltpu.HBM) for value in values]


def slopes_kernel(part, cols_ref, inverse_hbm, first_hbm, emb_hbm, left_hbm, right_hbm, out_ref, keep_ref, send_ref, grad_ref, inverse_ref, first_ref, emb_ref, own_ref, left_ref, right_ref, sems):
    rows, chunk = out_ref.shape[0], 96
    width = out_ref.shape[1]
    depth = left_ref.shape[1]
    loads = [
        (left_hbm, left_ref),
        (right_hbm.at[pl.ds(2 * rows if part == 0 else 0, depth), :], right_ref),
        (emb_hbm.at[pl.ds((1 - part) * rows, rows), :], emb_ref),
        (first_hbm, first_ref),
        (inverse_hbm.at[pl.ds(part * rows, rows), :], inverse_ref),
        (emb_hbm.at[pl.ds(part * rows, rows), :], own_ref),
    ]
    loads = [pltpu.make_async_copy(*load, sems.at[i]) for i, load in enumerate(loads)]
    for load in loads:
        load.start()
    for load in loads[:2]:
        load.wait()
    grad_ref[...] = jnp.dot(left_ref[...], right_ref[...], preferred_element_type=F32)
    for load in loads[2:]:
        load.wait()

    def some(i, _):
        at = pl.ds(pl.multiple_of(i * chunk, chunk), chunk)
        grad = first_ref[at, :1] * emb_ref[at, :].astype(F32) + grad_ref[at, :]
        values = own_ref[at, :].astype(F32)
        along = jnp.mean(grad * values, axis=-1, keepdims=True)
        out_ref[at, :] = (inverse_ref[at, :1] * (grad - values * along)).astype(BF16)
        return 0

    lax.fori_loop(0, rows // chunk, some, 0)
    for k in range(width // BLOCK // 2):
        for row, ref in ((0, keep_ref), (1, send_ref)):
            col = pl.multiple_of(cols_ref[row, k] * BLOCK, BLOCK)
            ref[:, pl.ds(k * BLOCK, BLOCK)] = out_ref[:, pl.ds(col, BLOCK)]


def slopes_of(part, cols, inverse, first, emb, left, right):
    rows = first.shape[0]
    width = emb.shape[1]
    anywhere = pl.BlockSpec(memory_space=pl.ANY)
    return pl.pallas_call(
        lambda *refs: slopes_kernel(part, *refs),
        in_specs=[pl.BlockSpec(memory_space=pltpu.SMEM)] + [anywhere] * 5,
        out_specs=vmem(3),
        out_shape=[
            jax.ShapeDtypeStruct((rows, width), BF16),
            jax.ShapeDtypeStruct((rows, width // 2), BF16),
            jax.ShapeDtypeStruct((rows, width // 2), BF16),
        ],
        scratch_shapes=[
            pltpu.VMEM((rows, width), F32),
            pltpu.VMEM(first.shape, F32),
            pltpu.VMEM(first.shape, F32),
            pltpu.VMEM((rows, width), BF16),
            pltpu.VMEM((rows, width), BF16),
            pltpu.VMEM(left.shape, BF16),
            pltpu.VMEM((left.shape[1], width), BF16),
            pltpu.SemaphoreType.DMA((6,)),
        ],
        compiler_params=pltpu.CompilerParams(vmem_limit_bytes=16 * 1024 * 1024),
        name="slopes_of",
    )(cols, *keep_far(inverse, first, emb, left), right)


def input_grad_kernel(count, *refs):
    slopes_refs, head_ref, out_refs = refs[:count], refs[count], refs[-count:]
    rows = slopes_refs[0].shape[0]
    slopes = jnp.concatenate([ref[...] for ref in slopes_refs], axis=0)
    grads = dot(slopes, head_ref[...], ((1,), (1,))).astype(BF16)
    for i, ref in enumerate(out_refs):
        ref[...] = grads[i * rows : (i + 1) * rows]


def input_grad(slopes, head, part, filled=()):
    count = len(slopes)
    rows, width = slopes[0].shape
    depth = head.shape[0]
    steps = depth // 512 // 2
    return pl.pallas_call(
        lambda *refs: input_grad_kernel(count, *refs),
        grid=(steps,),
        in_specs=[pl.BlockSpec((rows, width), lambda k: (0, 0))] * count
        + [pl.BlockSpec((512, width), lambda k: (k + part * steps, 0))]
        + [pl.BlockSpec(memory_space=pl.ANY)] * len(filled),
        out_specs=[pl.BlockSpec((rows, 512), lambda k: (0, k + part * steps))] * count,
        out_shape=[jax.ShapeDtypeStruct((rows, depth), BF16)] * count,
        input_output_aliases={count + 1 + i: i for i in range(len(filled))},
        compiler_params=pltpu.CompilerParams(vmem_limit_bytes=20 * 1024 * 1024),
        cost_estimate=pl.CostEstimate(flops=1, transcendentals=0, bytes_accessed=1),
        name="input_grad",
    )(*slopes, *keep_far(head), *filled)


def partial_kernel(outs, adds, at_ref, states_ref, slopes_ref, *refs):
    for i in range(outs):

        def block(k, _, i=i):
            row = pl.multiple_of(at_ref[2 * i + k] * BLOCK, BLOCK)
            part = pl.ds(pl.multiple_of(k * BLOCK, BLOCK), BLOCK)
            total = jnp.dot(
                states_ref[pl.ds(row, BLOCK), :], slopes_ref[...], preferred_element_type=F32
            ) * (1.0 / 128.0)
            for ref in refs[i * adds : (i + 1) * adds]:
                total = total + ref[part, :].astype(F32)
            refs[outs * adds + i][part, :] = total.astype(BF16)
            return 0

        lax.fori_loop(0, 2, block, 0)


def head_partial(states, slopes, at, adds):
    outs, width = len(adds), slopes.shape[1]
    return pl.pallas_call(
        lambda *refs: partial_kernel(outs, len(adds[0]), *refs),
        in_specs=[pl.BlockSpec(memory_space=pltpu.SMEM)] + vmem(2 + outs * len(adds[0])),
        out_specs=vmem(outs),
        out_shape=[jax.ShapeDtypeStruct((2 * BLOCK, width), BF16)] * outs,
        compiler_params=pltpu.CompilerParams(vmem_limit_bytes=20 * 1024 * 1024),
        name="head_partial",
    )(at, *keep_near(states), slopes, *[value for some in adds for value in some])


def add(*values):
    total = values[0].astype(F32)
    for value in values[1:]:
        total = total + value.astype(F32)
    return total.astype(BF16)


def scatter_head(states, slopes, core, head, query_dy, passage_dy, query_grads):
    def part(d1s, d2s, adds):
        at = [block_at(core, d1, d2) for d1, some in zip(d1s, d2s) for d2 in some]
        return head_partial(states, slopes, jnp.stack(at).astype(jnp.int32), adds)

    a, b = (2, 1), (-1, 0)
    far_a, far_b = part((2, 2), (a, b), ((), ()))
    far_a, far_b = shift(far_a, 1, 1), shift(far_b, 1, -1)
    up_b, down_a = part((1, -1), (b, a), ((), ()))
    up_b, down_a, passage_dy = together(up_b, down_a, passage_dy)
    up_b, down_a = shift(up_b, 1, 1), shift(down_a, 1, -1)
    (passage_grads,) = input_grad([passage_dy], head, 0)
    far_a, far_b, passage_grads = together(far_a, far_b, passage_grads)
    up_a, down_b = part((1, -1), (a, b), ((far_a,), (far_b,)))
    up_a, down_b = shift(up_a, 1, 1), shift(down_b, 1, -1)
    mine_a, mine_b = part((0, 0), (a, b), ((down_a,), (up_b,)))
    mine_a, mine_b, passage_dy = together(mine_a, mine_b, passage_dy)
    grads = input_grad([query_dy, passage_dy], head, 1, [query_grads, passage_grads])
    up_a, down_b, mine_a, mine_b, *grads = together(up_a, down_b, mine_a, mine_b, *grads)
    half = BLOCK // 2
    far, up = mine_a[:BLOCK], mine_a[BLOCK:]
    down, mine = mine_b[:BLOCK], mine_b[BLOCK:]
    up_far, up_up = up_a[:BLOCK], up_a[BLOCK:]
    down_down, down_mine = down_b[:BLOCK], down_b[BLOCK:]
    far_a = shift(add(far[:half], up_far[:half]), 2, 1)
    far_b = shift(add(far[half:], up_far[half:]), 2, -1)
    up_b = shift(add(up[half:], up_up[half:]), 2, 1)
    down_a = shift(add(down[:half], down_down[:half]), 2, -1)
    far_a, far_b, up_b, down_a = together(far_a, far_b, up_b, down_a)
    up_a = shift(add(up[:half], up_up[:half], far_a), 2, 1)
    down_b = shift(add(down[half:], down_down[half:], far_b), 2, -1)
    up_a, down_b = together(up_a, down_b)
    total = jnp.concatenate(
        [
            add(mine[:half], down_mine[:half], down_a, up_a),
            add(mine[half:], down_mine[half:], up_b, down_b),
        ],
        axis=0,
    )
    arrived = together(
        *[
            lax.ppermute(
                total[:, step * BLOCK : (step + 1) * BLOCK],
                "x",
                [(i, (i + step) % RING) for i in range(RING)],
            )
            for step in (2, 1, 3)
        ]
    )
    out = total[:, :BLOCK].astype(F32)
    for value in arrived:
        out = out + value.astype(F32)
    return out, *grads


def dot(a, b, contract=((1,), (0,))):
    return lax.dot_general(a, b, (contract, ((), ())), preferred_element_type=F32)


def per_device(queries, passages, head_weight, send_lists, neg_slots):
    core, x = lax.axis_index("c"), lax.axis_index("x")
    rows_dev, depth = queries.shape
    width = head_weight.shape[1]
    groups, capacity = send_lists.shape[2], send_lists.shape[3]
    slot_count = groups * capacity
    flat_lists = send_lists.reshape(slot_count)

    owner = (flat_lists[None, :] == jnp.arange(rows_dev, dtype=jnp.int32)[:, None]).astype(BF16)
    own = lax.dynamic_slice_in_dim(head_weight, core * (width // 2), width // 2, axis=1)

    up, down = shift(own, 1, 1), shift(own, 1, -1)
    picked = dot(owner, passages, ((0,), (0,))).astype(BF16).reshape(groups, capacity, depth)
    own, picked = together(own, picked)
    own_up, own_down = shift(own, 2, 1), shift(own, 2, -1)
    arrived = lax.all_to_all(picked, ("x", "c"), split_axis=0, concat_axis=0, tiled=True)
    arrived = arrived.reshape(slot_count, depth)

    far = shift(up, 1, 1)
    up_up, up_down = shift(up, 2, 1), shift(up, 2, -1)
    slot_ids = jnp.arange(slot_count, dtype=jnp.int32)[None, :]
    counts = jnp.zeros((rows_dev, slot_count), F32)
    for j in range(neg_slots.shape[1]):
        counts = counts + (neg_slots[:, j : j + 1] == slot_ids).astype(F32)
    far, up_up, up_down, own_up, own_down, counts, owner = together(
        far, up_up, up_down, own_up, own_down, counts, owner
    )

    second = jnp.concatenate([down, far], axis=0)
    second_up, second_down = shift(second, 2, 1), shift(second, 2, -1)
    first_up = jnp.concatenate([own_up, up_up], axis=0)
    early = [own, up, second, first_up, own_down, up_down]
    early = early, [swap(piece) for piece in early]
    places = [(0, 0), (-1, 0), (1, 0), (2, 0), (0, -1), (-1, -1), (0, 1), (-1, 1)]
    places += [(1, -1), (2, -1), (1, 1), (2, 1), (0, 2), (-1, 2), (1, 2), (2, 2)]
    at = [block_at(core, *place) for place in places] + [block_at(1 - core, *place) for place in places]
    side = [core, 1 - core] + [core] * 30
    at = jnp.stack([jnp.stack(at), jnp.stack(side)]).astype(jnp.int32)
    xs = queries, passages, arrived
    head, part = project_early(at, xs[:2], early[0] + early[1])
    second_up, second_down, first_up, part = together(second_up, second_down, first_up, part)

    first_far, second_far = shift(first_up, 2, 1), shift(second_down, 2, -1)
    middle = [second_up, second_down]
    other_middle = [swap(piece) for piece in middle]
    head, part = project_middle(at, 8, xs, early[0] + middle + early[1] + other_middle, part, head)
    first_far, second_far, part = together(first_far, second_far, part)
    late = [first_far, second_far, swap(first_far), swap(second_far)]
    head, emb, inverse, mixing, first, fetched_grad = project_last(at, xs, late, part, counts, head)
    returned = lax.all_to_all(
        fetched_grad.reshape(groups, capacity, width),
        ("x", "c"),
        split_axis=0,
        concat_axis=0,
        tiled=True,
    ).reshape(slot_count, width)

    to_x = [(x + step) % RING for step in range(RING)]
    cols = jnp.stack(
        [jnp.stack([2 * to + core for to in to_x]), jnp.stack([2 * to + 1 - core for to in to_x])]
    ).astype(jnp.int32)
    query_states, passage_states, first = together(queries, passages, first)
    query_dy, query_keep, query_send = slopes_of(0, cols, inverse, first, emb, mixing, emb)
    turned = turn(query_states, passage_states, swap(query_states), swap(passage_states))
    (query_grads,) = input_grad([query_dy], head, 0)
    returned, query_grads, query_send, turned = together(returned, query_grads, query_send, turned)
    query_other = swap(query_send)

    passage_dy, passage_keep, passage_send = slopes_of(
        1, cols, inverse, first, emb, owner, returned
    )
    passage_other = swap(passage_send)
    slopes = jnp.concatenate([query_keep, passage_keep, query_other, passage_other], axis=0)
    head_grads, query_grads, passage_grads = scatter_head(
        turned, slopes, core, head, query_dy, passage_dy, query_grads
    )
    return (query_grads, passage_grads, head_grads)


def solution(mesh):
    fine = Mesh(mesh.devices.reshape(4, 2, 4, 4), ("x", "c", "y", "z"))
    every = ("x", "c", "y", "z")
    return jax.shard_map(
        per_device,
        mesh=fine,
        in_specs=(
            P(every, None),
            P(every, None),
            P(("y", "z"), None),
            P(("x", "c"), ("y", "z"), None, None),
            P(every, None),
        ),
        out_specs=(P(every, None), P(every, None), P(("y", "z"), ("x", "c"))),
        check_vma=False,
    )
```

profile of v0, /device:TPU:0, one launch (start us, length us, event | category | flops | bytes accessed | tf_op | source)
XLA Modules:
  0.0 198.7 jit_solution(4189259194621593635)
XLA Ops:
  5.1 4.1 %convolution_convert_fusion = bf16[384,4096]{1,0:T(8,128)(2,1)} fusion(bf16[192,4096]{1,0:T(8,128)(2,1)} %refs_1_.6, s32[384]{0:T(512)S(1)} %eq.458), kind=kOutput, calls=%fused_computation | convolution fusion | flops 605626368 | bytes 4720128 | tf_op jit(solution)/shard_map/dot_general | solution.py:586
  14.9 4.3 %all-to-all-start = ((bf16[8,48,4096]{2,1,0:T(8,128)(2,1)}), bf16[8,48,4096]{2,1,0:T(8,128)(2,1)S(1)}, u32[]{:S(2)}, u32[]{:S(2)}) async-start(bf16[8,48,4096]{2,1,0:T(8,128)(2,1)} %bitcast.70), calls=%async_computation | async-start | bytes 6291456 | tf_op jit(solution)/shard_map/all_to_all | solution.py:604
  29.3 5.9 %collective-permute-done.2 = bf16[256,1024]{1,0:T(8,128)(2,1)S(1)} collective-permute-done((bf16[256,1024]{1,0:T(8,128)(2,1)}, bf16[256,1024]{1,0:T(8,128)(2,1)S(1)}, u32[]{:S(2)}, u32[]{:S(2)}) %collective-permute-start.2) | collective-permute-done | bytes 524320 | tf_op jit(solution)/shard_map/ppermute | solution.py:27
  39.3 3.1 %collective-permute-start.8 = (bf16[512,1024]{1,0:T(8,128)(2,1)}, bf16[512,1024]{1,0:T(8,128)(2,1)}, u32[]{:S(2)}, u32[]{:S(2)}) collective-permute-start(bf16[512,1024]{1,0:T(8,128)(2,1)} %constant_dynamic-update-slice_fusion.refs_5_.refs_6_), channel_id=1, source_target_pairs={{0,3},{1,0},{2,1},{3,2},{4,7},{5,4},{6,5},{7,6},{8,11},{9,8},{10,9... | collective-permute-start | bytes 3145736 | tf_op jit(solution)/shard_map/ppermute | solution.py:27
  44.7 10.2 %project_early.1 = (bf16[4096,2048]{1,0:T(8,128)(2,1)}, bf16[384,2048]{1,0:T(8,128)(2,1)}) custom-call(s32[2,32]{1,0:T(2,128)S(1)} %pad_add_fusion.refs_0_, bf16[192,4096]{1,0:T(8,128)(2,1)} %refs_0_, bf16[192,4096]{1,0:T(8,128)(2,1)} %refs_1_.6, bf16[256,1024]{1,0:T(8,128)(2,1)} %constant_dynamic-slice_fusion.refs_3_.refs_4_, ...), custom_call_target="tpu_custom_call" | custom-call | tf_op jit(solution)/shard_map/project_early/pallas_call | solution.py:180
  60.9 15.4 %project_middle.1 = (bf16[4096,2048]{1,0:T(8,128)(2,1)}, bf16[768,2048]{1,0:T(8,128)(2,1)}) custom-call(s32[2,32]{1,0:T(2,128)S(1)} %pad_add_fusion.refs_0_, bf16[192,4096]{1,0:T(8,128)(2,1)} %refs_0_, bf16[192,4096]{1,0:T(8,128)(2,1)} %refs_1_.6, bf16[384,4096]{1,0:T(8,128)(2,1)} %bitcast.68, ...), custom_call_target="tpu_custom_call", output_to_operand_aliasing={{0}: (21, {})} | custom-call | tf_op jit(solution)/shard_map/project_middle/pallas_call | solution.py:250
  81.7 13.0 %project_last.1 = (bf16[4096,2048]{1,0:T(8,128)(2,1)}, bf16[768,2048]{1,0:T(8,128)(2,1)}, f32[768,128]{1,0:T(8,128)}, bf16[192,384]{1,0:T(8,128)(2,1)}, f32[192,128]{1,0:T(8,128)}, /*index=5*/bf16[384,2048]{1,0:T(8,128)(2,1)}) custom-call(s32[2,32]{1,0:T(2,128)S(1)} %pad_add_fusion.refs_0_, ...), custom_call_target="tpu_custom_call", output_to_operand_aliasing={{0}: (10, {})} | custom-call | tf_op jit(solution)/shard_map/project_last/pallas_call | solution.py:316
  95.3 4.4 %all-to-all-start.1 = ((bf16[8,48,2048]{2,1,0:T(8,128)(2,1)}), bf16[8,48,2048]{2,1,0:T(8,128)(2,1)S(1)}, u32[]{:S(2)}, u32[]{:S(2)}) async-start(bf16[8,48,2048]{2,1,0:T(8,128)(2,1)} %bitcast.71), calls=%async_computation.1 | async-start | bytes 3145728 | tf_op jit(solution)/shard_map/all_to_all | solution.py:638
  99.9 3.4 %slopes_of.2 = (bf16[192,2048]{1,0:T(8,128)(2,1)S(1)}, bf16[192,1024]{1,0:T(8,128)(2,1)S(1)}, bf16[192,1024]{1,0:T(8,128)(2,1)S(1)}) custom-call(s32[2,4]{1,0:T(2,128)S(1)} %pad_add_fusion.1.refs_0_, f32[768,128]{1,0:T(8,128)} %get-tuple-element.96.refs_1_, f32[192,128]{1,0:T(8,128)} %get-tuple-element.98.refs_2_, ...), custom_call_target="tpu_custom_call" | custom-call | tf_op jit(solution)/shard_map/slopes_of/pallas_call | solution.py:441
  103.3 6.7 %input_grad.3.refs_3_ = bf16[192,4096]{1,0:T(8,128)(2,1)} custom-call(bf16[192,2048]{1,0:T(8,128)(2,1)S(1)} %get-tuple-element.101.refs_0_, bf16[4096,2048]{1,0:T(8,128)(2,1)} %get-tuple-element.102.refs_1_.refs_2_), custom_call_target="tpu_custom_call" | custom-call | flops 1 | bytes 1 | tf_op jit(solution)/shard_map/input_grad/pallas_call | solution.py:479
  109.9 4.8 %turn.1.refs_1_ = bf16[4096,768]{1,0:T(8,128)(2,1)} custom-call(bf16[192,4096]{1,0:T(8,128)(2,1)} %refs_0_, bf16[192,4096]{1,0:T(8,128)(2,1)} %refs_1_.6, bf16[192,4096]{1,0:T(8,128)(2,1)} %collective-permute-done.21.refs_2_, bf16[192,4096]{1,0:T(8,128)(2,1)} %collective-permute-done.22.refs_3_), custom_call_target="tpu_custom_call" | custom-call | flops 1 | bytes 1 | tf_op jit(solution)/shard_map/turn/pallas_call | solution.py:75
  114.7 6.6 %all-to-all-done.1 = bf16[8,48,2048]{2,1,0:T(8,128)(2,1)S(1)} async-done(((bf16[8,48,2048]{2,1,0:T(8,128)(2,1)}), bf16[8,48,2048]{2,1,0:T(8,128)(2,1)S(1)}, u32[]{:S(2)}, u32[]{:S(2)}) %all-to-all-start.1) | async-done | bytes 1572896 | tf_op jit(solution)/shard_map/all_to_all | solution.py:638
  121.4 3.1 %slopes_of.3 = (bf16[192,2048]{1,0:T(8,128)(2,1)S(1)}, bf16[192,1024]{1,0:T(8,128)(2,1)S(1)}, bf16[192,1024]{1,0:T(8,128)(2,1)S(1)}) custom-call(s32[2,4]{1,0:T(2,128)S(1)} %pad_add_fusion.1.refs_0_, f32[768,128]{1,0:T(8,128)} %get-tuple-element.96.refs_1_, f32[192,128]{1,0:T(8,128)} %get-tuple-element.98.refs_2_, ...), custom_call_target="tpu_custom_call" | custom-call | tf_op jit(solution)/shard_map/slopes_of/pallas_call | solution.py:441
  129.6 3.0 %collective-permute-start.26 = (bf16[512,1024]{1,0:T(8,128)(2,1)S(1)}, bf16[512,1024]{1,0:T(8,128)(2,1)S(1)}, u32[]{:S(2)}, u32[]{:S(2)}) collective-permute-start(bf16[512,1024]{1,0:T(8,128)(2,1)S(1)} %get-tuple-element.114), channel_id=1, source_target_pairs={{0,12},{1,13},{2,14},{3,15},{4,0},{5,1},{6,2},{7,3},{8,4},{9,5},{1... | collective-permute-start | bytes 3145736 | tf_op jit(solution)/shard_map/ppermute | solution.py:27
  137.7 6.7 %input_grad.4.refs_4_ = bf16[192,4096]{1,0:T(8,128)(2,1)} custom-call(bf16[192,2048]{1,0:T(8,128)(2,1)S(1)} %get-tuple-element.129.refs_0_.refs_1_, bf16[4096,2048]{1,0:T(8,128)(2,1)} %get-tuple-element.102.refs_1_.refs_2_), custom_call_target="tpu_custom_call" | custom-call | flops 1 | bytes 1 | tf_op jit(solution)/shard_map/input_grad/pallas_call | solution.py:479
  145.4 2.9 %head_partial.6 = (bf16[512,1024]{1,0:T(8,128)(2,1)S(1)}, bf16[512,1024]{1,0:T(8,128)(2,1)S(1)}) custom-call(s32[4]{0:T(128)S(1)} %pad_add_fusion.2.refs_0_, bf16[4096,768]{1,0:T(8,128)(2,1)S(1)} %copy-done.2, bf16[768,1024]{1,0:T(8,128)(2,1)S(1)} %constant_dynamic-update-slice_fusion.4.refs_2_, bf16[512,1024]{1,0:T(8,128)(2,1)S(1)} %collective-permute-done.25.refs_3_, ...), custom_call_target="tpu_custom_call" | custom-call | tf_op jit(solution)/shard_map/head_partial/pallas_call | solution.py:513
  151.7 4.4 %collective-permute-done.29.refs_3_ = bf16[512,1024]{1,0:T(8,128)(2,1)S(1)} collective-permute-done((bf16[512,1024]{1,0:T(8,128)(2,1)S(1)}, bf16[512,1024]{1,0:T(8,128)(2,1)S(1)}, u32[]{:S(2)}, u32[]{:S(2)}) %collective-permute-start.29) | collective-permute-done | bytes 1048608 | tf_op jit(solution)/shard_map/ppermute | solution.py:27
  156.6 2.9 %head_partial.7 = (bf16[512,1024]{1,0:T(8,128)(2,1)S(1)}, bf16[512,1024]{1,0:T(8,128)(2,1)S(1)}) custom-call(s32[4]{0:T(128)S(1)} %pad_add_fusion.5.refs_0_, bf16[4096,768]{1,0:T(8,128)(2,1)S(1)} %copy-done.2, bf16[768,1024]{1,0:T(8,128)(2,1)S(1)} %constant_dynamic-update-slice_fusion.4.refs_2_, bf16[512,1024]{1,0:T(8,128)(2,1)S(1)} %collective-permute-done.29.refs_3_, ...), custom_call_target="tpu_custom_call" | custom-call | tf_op jit(solution)/shard_map/head_partial/pallas_call | solution.py:513
  159.5 7.2 %input_grad.5 = (bf16[192,4096]{1,0:T(8,128)(2,1)}, bf16[192,4096]{1,0:T(8,128)(2,1)}) custom-call(bf16[192,2048]{1,0:T(8,128)(2,1)S(1)} %get-tuple-element.101.refs_0_, bf16[192,2048]{1,0:T(8,128)(2,1)S(1)} %get-tuple-element.129.refs_0_.refs_1_, ...), custom_call_target="tpu_custom_call", output_to_operand_aliasing={{0}: (3, {}), {1}: (4, {})} | custom-call | flops 1 | bytes 1 | tf_op jit(solution)/shard_map/input_grad/pallas_call | solution.py:479
  170.7 3.2 %collective-permute-start.32 = (bf16[128,1024]{1,0:T(8,128)(2,1)S(1)}, bf16[128,1024]{1,0:T(8,128)(2,1)S(1)}, u32[]{:S(2)}, u32[]{:S(2)}) collective-permute-start(bf16[128,1024]{1,0:T(8,128)(2,1)S(1)} %get-tuple-element.152), channel_id=1, source_target_pairs={{0,3},{1,0},{2,1},{3,2},{4,7},{5,4},{6,5},{7,6},{8,11},{9,8},{10,9... | collective-permute-start | bytes 786440 | tf_op jit(solution)/shard_map/ppermute | solution.py:27
  174.4 3.9 %collective-permute-done.31 = bf16[128,1024]{1,0:T(8,128)(2,1)S(1)} collective-permute-done((bf16[128,1024]{1,0:T(8,128)(2,1)S(1)}, bf16[128,1024]{1,0:T(8,128)(2,1)S(1)}, u32[]{:S(2)}, u32[]{:S(2)}) %collective-permute-start.31) | collective-permute-done | bytes 262176 | tf_op jit(solution)/shard_map/ppermute | solution.py:27
  178.3 3.2 %collective-permute-done.33 = bf16[128,1024]{1,0:T(8,128)(2,1)S(1)} collective-permute-done((bf16[128,1024]{1,0:T(8,128)(2,1)S(1)}, bf16[128,1024]{1,0:T(8,128)(2,1)S(1)}, u32[]{:S(2)}, u32[]{:S(2)}) %collective-permute-start.33) | collective-permute-done | bytes 262176 | tf_op jit(solution)/shard_map/ppermute | solution.py:27
  183.9 4.1 %collective-permute-done.36 = bf16[128,1024]{1,0:T(8,128)(2,1)S(1)} collective-permute-done((bf16[128,1024]{1,0:T(8,128)(2,1)S(1)}, bf16[128,1024]{1,0:T(8,128)(2,1)S(1)}, u32[]{:S(2)}, u32[]{:S(2)}) %collective-permute-start.36) | collective-permute-done | bytes 262176 | tf_op jit(solution)/shard_map/ppermute | solution.py:27
  193.6 3.0 %collective-permute-done.37 = bf16[256,256]{1,0:T(8,128)(2,1)S(1)} collective-permute-done((bf16[256,256]{1,0:T(8,128)(2,1)S(1)}, bf16[256,256]{1,0:T(8,128)(2,1)S(1)}, u32[]{:S(2)}, u32[]{:S(2)}) %collective-permute-start.37) | collective-permute-done | bytes 131104 | tf_op jit(solution)/shard_map/ppermute | solution.py:571
  (117 shorter events, 68.3 us)
Async XLA Ops:
  2.7 16.5 %collective-permute-start.1 = (bf16[256,1024]{1,0:T(8,128)(2,1)}, bf16[256,1024]{1,0:T(8,128)(2,1)}, u32[]{:S(2)}, u32[]{:S(2)}) collective-permute-start(bf16[256,1024]{1,0:T(8,128)(2,1)} %constant_dynamic-slice_fusion.refs_3_.refs_4_), channel_id=1, source_target_pairs={{0,4},{1,5},{2,6},{3,7},{4,8},{5,9},{6,10},{7,11},{8,12},{9,13},{1... | collective-permute-start | bytes 1572872 | tf_op jit(solution)/shard_map/ppermute | solution.py:27
  9.2 11.5 %collective-permute-start.5 = (bf16[256,1024]{1,0:T(8,128)(2,1)}, bf16[256,1024]{1,0:T(8,128)(2,1)}, u32[]{:S(2)}, u32[]{:S(2)}) collective-permute-start(bf16[256,1024]{1,0:T(8,128)(2,1)} %constant_dynamic-slice_fusion.refs_3_.refs_4_), channel_id=1, source_target_pairs={{0,1},{1,2},{2,3},{3,0},{4,5},{5,6},{6,7},{7,4},{8,9},{9,10},{10,1... | collective-permute-start | bytes 1572872 | tf_op jit(solution)/shard_map/ppermute | solution.py:27
  11.1 15.1 %collective-permute-start.6 = (bf16[256,1024]{1,0:T(8,128)(2,1)}, bf16[256,1024]{1,0:T(8,128)(2,1)}, u32[]{:S(2)}, u32[]{:S(2)}) collective-permute-start(bf16[256,1024]{1,0:T(8,128)(2,1)} %constant_dynamic-slice_fusion.refs_3_.refs_4_), channel_id=1, source_target_pairs={{0,3},{1,0},{2,1},{3,2},{4,7},{5,4},{6,5},{7,6},{8,11},{9,8},{10,9... | collective-permute-start | bytes 1572872 | tf_op jit(solution)/shard_map/ppermute | solution.py:27
  13.2 12.9 %collective-permute-start = (bf16[256,1024]{1,0:T(8,128)(2,1)}, bf16[256,1024]{1,0:T(8,128)(2,1)}, u32[]{:S(2)}, u32[]{:S(2)}) collective-permute-start(bf16[256,1024]{1,0:T(8,128)(2,1)} %constant_dynamic-slice_fusion.refs_3_.refs_4_), channel_id=1, source_target_pairs={{0,12},{1,13},{2,14},{3,15},{4,0},{5,1},{6,2},{7,3},{8,4},{9,5},{1... | collective-permute-start | bytes 1572872 | tf_op jit(solution)/shard_map/ppermute | solution.py:27
  14.9 44.4 %all-to-all-start = ((bf16[8,48,4096]{2,1,0:T(8,128)(2,1)}), bf16[8,48,4096]{2,1,0:T(8,128)(2,1)S(1)}, u32[]{:S(2)}, u32[]{:S(2)}) async-start(bf16[8,48,4096]{2,1,0:T(8,128)(2,1)} %bitcast.70), calls=%async_computation | async-start | bytes 6291456 | tf_op jit(solution)/shard_map/all_to_all | solution.py:604
  19.2 15.9 %collective-permute-start.2 = (bf16[256,1024]{1,0:T(8,128)(2,1)}, bf16[256,1024]{1,0:T(8,128)(2,1)S(1)}, u32[]{:S(2)}, u32[]{:S(2)}) collective-permute-start(bf16[256,1024]{1,0:T(8,128)(2,1)} %collective-permute-done.1.refs_4_.refs_5_), channel_id=1, source_target_pairs={{0,4},{1,5},{2,6},{3,7},{4,8},{5,9},{6,10},{7,11},{8,12},{9,13},{1... | collective-permute-start | bytes 1572872 | tf_op jit(solution)/shard_map/ppermute | solution.py:27
  19.7 15.5 %collective-permute-start.3 = (bf16[256,1024]{1,0:T(8,128)(2,1)}, bf16[256,1024]{1,0:T(8,128)(2,1)S(1)}, u32[]{:S(2)}, u32[]{:S(2)}) collective-permute-start(bf16[256,1024]{1,0:T(8,128)(2,1)} %collective-permute-done.1.refs_4_.refs_5_), channel_id=1, source_target_pairs={{0,1},{1,2},{2,3},{3,0},{4,5},{5,6},{6,7},{7,4},{8,9},{9,10},{10,1... | collective-permute-start | bytes 1572872 | tf_op jit(solution)/shard_map/ppermute | solution.py:27
  20.7 14.4 %collective-permute-start.4 = (bf16[256,1024]{1,0:T(8,128)(2,1)}, bf16[256,1024]{1,0:T(8,128)(2,1)}, u32[]{:S(2)}, u32[]{:S(2)}) collective-permute-start(bf16[256,1024]{1,0:T(8,128)(2,1)} %collective-permute-done.1.refs_4_.refs_5_), channel_id=1, source_target_pairs={{0,3},{1,0},{2,1},{3,2},{4,7},{5,4},{6,5},{7,6},{8,11},{9,8},{10,9... | collective-permute-start | bytes 1572872 | tf_op jit(solution)/shard_map/ppermute | solution.py:27
  26.2 13.0 %collective-permute-start.9 = (bf16[256,1024]{1,0:T(8,128)(2,1)}, bf16[256,1024]{1,0:T(8,128)(2,1)}, u32[]{:S(2)}, u32[]{:S(2)}) collective-permute-start(bf16[256,1024]{1,0:T(8,128)(2,1)} %constant_dynamic-slice_fusion.refs_3_.refs_4_), channel_id=1, source_target_pairs={{0,16},{16,0},{1,17},{17,1},{2,18},{18,2},{3,19},{19,3},{4,20},{20... | collective-permute-start | bytes 1572872 | tf_op jit(solution)/shard_map/ppermute | solution.py:31
  26.2 13.1 %collective-permute-start.10 = (bf16[256,1024]{1,0:T(8,128)(2,1)}, bf16[256,1024]{1,0:T(8,128)(2,1)}, u32[]{:S(2)}, u32[]{:S(2)}) collective-permute-start(bf16[256,1024]{1,0:T(8,128)(2,1)} %collective-permute-done.1.refs_4_.refs_5_), channel_id=1, source_target_pairs={{0,16},{16,0},{1,17},{17,1},{2,18},{18,2},{3,19},{19,3},{4,20},{20... | collective-permute-start | bytes 1572872 | tf_op jit(solution)/shard_map/ppermute | solution.py:31
  39.2 16.3 %collective-permute-start.7 = (bf16[512,1024]{1,0:T(8,128)(2,1)}, bf16[512,1024]{1,0:T(8,128)(2,1)}, u32[]{:S(2)}, u32[]{:S(2)}) collective-permute-start(bf16[512,1024]{1,0:T(8,128)(2,1)} %constant_dynamic-update-slice_fusion.refs_5_.refs_6_), channel_id=1, source_target_pairs={{0,1},{1,2},{2,3},{3,0},{4,5},{5,6},{6,7},{7,4},{8,9},{9,10},{10,1... | collective-permute-start | bytes 3145736 | tf_op jit(solution)/shard_map/ppermute | solution.py:27
  39.3 16.2 %collective-permute-start.8 = (bf16[512,1024]{1,0:T(8,128)(2,1)}, bf16[512,1024]{1,0:T(8,128)(2,1)}, u32[]{:S(2)}, u32[]{:S(2)}) collective-permute-start(bf16[512,1024]{1,0:T(8,128)(2,1)} %constant_dynamic-update-slice_fusion.refs_5_.refs_6_), channel_id=1, source_target_pairs={{0,3},{1,0},{2,1},{3,2},{4,7},{5,4},{6,5},{7,6},{8,11},{9,8},{10,9... | collective-permute-start | bytes 3145736 | tf_op jit(solution)/shard_map/ppermute | solution.py:27
  56.0 20.2 %collective-permute-start.15 = (bf16[512,1024]{1,0:T(8,128)(2,1)}, bf16[512,1024]{1,0:T(8,128)(2,1)}, u32[]{:S(2)}, u32[]{:S(2)}) collective-permute-start(bf16[512,1024]{1,0:T(8,128)(2,1)} %constant_dynamic-update-slice_fusion.2.refs_6_.refs_7_), channel_id=1, source_target_pairs={{0,1},{1,2},{2,3},{3,0},{4,5},{5,6},{6,7},{7,4},{8,9},{9,10},{10,1... | collective-permute-start | bytes 3145736 | tf_op jit(solution)/shard_map/ppermute | solution.py:27
  56.9 19.4 %collective-permute-start.16 = (bf16[512,1024]{1,0:T(8,128)(2,1)}, bf16[512,1024]{1,0:T(8,128)(2,1)}, u32[]{:S(2)}, u32[]{:S(2)}) collective-permute-start(bf16[512,1024]{1,0:T(8,128)(2,1)} %collective-permute-done.8.refs_11_), channel_id=1, source_target_pairs={{0,3},{1,0},{2,1},{3,2},{4,7},{5,4},{6,5},{7,6},{8,11},{9,8},{10,9... | collective-permute-start | bytes 3145736 | tf_op jit(solution)/shard_map/ppermute | solution.py:27
  94.7 15.2 %collective-permute-start.21 = (bf16[192,4096]{1,0:T(8,128)(2,1)}, bf16[192,4096]{1,0:T(8,128)(2,1)}, u32[]{:S(2)}, u32[]{:S(2)}) collective-permute-start(bf16[192,4096]{1,0:T(8,128)(2,1)} %refs_0_), channel_id=1, source_target_pairs={{0,16},{16,0},{1,17},{17,1},{2,18},{18,2},{3,19},{19,3},{4,20},{20... | collective-permute-start | bytes 4718600 | tf_op jit(solution)/shard_map/ppermute | solution.py:31
  95.0 15.0 %collective-permute-start.22 = (bf16[192,4096]{1,0:T(8,128)(2,1)}, bf16[192,4096]{1,0:T(8,128)(2,1)}, u32[]{:S(2)}, u32[]{:S(2)}) collective-permute-start(bf16[192,4096]{1,0:T(8,128)(2,1)} %refs_1_.6), channel_id=1, source_target_pairs={{0,16},{16,0},{1,17},{17,1},{2,18},{18,2},{3,19},{19,3},{4,20},{20... | collective-permute-start | bytes 4718600 | tf_op jit(solution)/shard_map/ppermute | solution.py:31
  95.3 26.0 %all-to-all-start.1 = ((bf16[8,48,2048]{2,1,0:T(8,128)(2,1)}), bf16[8,48,2048]{2,1,0:T(8,128)(2,1)S(1)}, u32[]{:S(2)}, u32[]{:S(2)}) async-start(bf16[8,48,2048]{2,1,0:T(8,128)(2,1)} %bitcast.71), calls=%async_computation.1 | async-start | bytes 3145728 | tf_op jit(solution)/shard_map/all_to_all | solution.py:638
  129.3 16.1 %collective-permute-start.25 = (bf16[512,1024]{1,0:T(8,128)(2,1)S(1)}, bf16[512,1024]{1,0:T(8,128)(2,1)S(1)}, u32[]{:S(2)}, u32[]{:S(2)}) collective-permute-start(bf16[512,1024]{1,0:T(8,128)(2,1)S(1)} %get-tuple-element.113), channel_id=1, source_target_pairs={{0,4},{1,5},{2,6},{3,7},{4,8},{5,9},{6,10},{7,11},{8,12},{9,13},{1... | collective-permute-start | bytes 3145736 | tf_op jit(solution)/shard_map/ppermute | solution.py:27
  129.6 15.7 %collective-permute-start.26 = (bf16[512,1024]{1,0:T(8,128)(2,1)S(1)}, bf16[512,1024]{1,0:T(8,128)(2,1)S(1)}, u32[]{:S(2)}, u32[]{:S(2)}) collective-permute-start(bf16[512,1024]{1,0:T(8,128)(2,1)S(1)} %get-tuple-element.114), channel_id=1, source_target_pairs={{0,12},{1,13},{2,14},{3,15},{4,0},{5,1},{6,2},{7,3},{8,4},{9,5},{1... | collective-permute-start | bytes 3145736 | tf_op jit(solution)/shard_map/ppermute | solution.py:27
  135.7 20.5 %collective-permute-start.29 = (bf16[512,1024]{1,0:T(8,128)(2,1)S(1)}, bf16[512,1024]{1,0:T(8,128)(2,1)S(1)}, u32[]{:S(2)}, u32[]{:S(2)}) collective-permute-start(bf16[512,1024]{1,0:T(8,128)(2,1)S(1)} %get-tuple-element.123), channel_id=1, source_target_pairs={{0,12},{1,13},{2,14},{3,15},{4,0},{5,1},{6,2},{7,3},{8,4},{9,5},{1... | collective-permute-start | bytes 3145736 | tf_op jit(solution)/shard_map/ppermute | solution.py:27
  136.3 20.3 %collective-permute-start.30 = (bf16[512,1024]{1,0:T(8,128)(2,1)S(1)}, bf16[512,1024]{1,0:T(8,128)(2,1)S(1)}, u32[]{:S(2)}, u32[]{:S(2)}) collective-permute-start(bf16[512,1024]{1,0:T(8,128)(2,1)S(1)} %get-tuple-element.124), channel_id=1, source_target_pairs={{0,4},{1,5},{2,6},{3,7},{4,8},{5,9},{6,10},{7,11},{8,12},{9,13},{1... | collective-permute-start | bytes 3145736 | tf_op jit(solution)/shard_map/ppermute | solution.py:27
  148.3 19.6 %collective-permute-start.27 = (bf16[512,1024]{1,0:T(8,128)(2,1)S(1)}, bf16[512,1024]{1,0:T(8,128)(2,1)S(1)}, u32[]{:S(2)}, u32[]{:S(2)}) collective-permute-start(bf16[512,1024]{1,0:T(8,128)(2,1)S(1)} %get-tuple-element.121), channel_id=1, source_target_pairs={{0,4},{1,5},{2,6},{3,7},{4,8},{5,9},{6,10},{7,11},{8,12},{9,13},{1... | collective-permute-start | bytes 3145736 | tf_op jit(solution)/shard_map/ppermute | solution.py:27
  149.0 18.8 %collective-permute-start.28 = (bf16[512,1024]{1,0:T(8,128)(2,1)S(1)}, bf16[512,1024]{1,0:T(8,128)(2,1)S(1)}, u32[]{:S(2)}, u32[]{:S(2)}) collective-permute-start(bf16[512,1024]{1,0:T(8,128)(2,1)S(1)} %get-tuple-element.122), channel_id=1, source_target_pairs={{0,12},{1,13},{2,14},{3,15},{4,0},{5,1},{6,2},{7,3},{8,4},{9,5},{1... | collective-permute-start | bytes 3145736 | tf_op jit(solution)/shard_map/ppermute | solution.py:27
  170.6 7.7 %collective-permute-start.31 = (bf16[128,1024]{1,0:T(8,128)(2,1)S(1)}, bf16[128,1024]{1,0:T(8,128)(2,1)S(1)}, u32[]{:S(2)}, u32[]{:S(2)}) collective-permute-start(bf16[128,1024]{1,0:T(8,128)(2,1)S(1)} %get-tuple-element.153), channel_id=1, source_target_pairs={{0,1},{1,2},{2,3},{3,0},{4,5},{5,6},{6,7},{7,4},{8,9},{9,10},{10,1... | collective-permute-start | bytes 786440 | tf_op jit(solution)/shard_map/ppermute | solution.py:27
  (25 other events, 125.7 us)
where the time goes:
time: 199 us
  Pallas kernels  81.9 us (41%)
  waiting for transfers between devices  49.1 us (25%)
  starting transfers between devices  48.9 us (25%)
  local copies, waits for them, and re-layouts  10.4 us (5%)
  matrix products  4.07 us (2%)
  other arithmetic  3.36 us (2%)
    ppermute x23, starting transfers between devices, shift(): return lax.ppermute(value, ('c', 'y', 'z'), pairs)  33.1 us
    ppermute x23, waiting for transfers between devices, shift(): return lax.ppermute(value, ('c', 'y', 'z'), pairs)  30.4 us
    pallas_call x3, Pallas kernels, input_grad(): pl.pallas_call(lambda *refs: input_grad_kernel(count, *refs), grid=(steps...  20.5 us
    pallas_call x1, Pallas kernels, project_middle(): pl.pallas_call(lambda *refs: project_middle_kernel(count, early, *refs),...  15.4 us
    pallas_call x1, Pallas kernels, project_last(): pl.pallas_call(lambda *refs: project_last_kernel(count, *refs), in_specs=...  13 us
    pallas_call x4, Pallas kernels, head_partial(): pl.pallas_call(lambda *refs: partial_kernel(outs, len(adds[0]), *refs), i...  11.6 us
    pallas_call x1, Pallas kernels, project_early(): pl.pallas_call(lambda *refs: project_early_kernel(count, *refs), in_specs...  10.2 us
    ppermute x14, waiting for transfers between devices, swap(): return lax.ppermute(value, 'c', SWAP)  7.78 us
  transfers between devices with their start and end apart: 42, of which 21 were waited for; matrix products, arithmetic and copies ran while one was open for 6% of the time, Pallas kernels for 33%

commit v1 on v0

--- a/solution.py
+++ b/solution.py
@@ -265,7 +265,7 @@
         input_output_aliases={len(ins): 0},
         compiler_params=pltpu.CompilerParams(vmem_limit_bytes=36 * 1024 * 1024),
         name="project_middle",
-    )(at, *keep_far(*xs, *pieces, part, head))
+    )(at, *keep_far(*xs), *pieces, *keep_far(part, head))
 
 
 def project_last_kernel(count, at_ref, *refs):
@@ -340,7 +340,7 @@
         input_output_aliases={len(ins): 0},
         compiler_params=pltpu.CompilerParams(vmem_limit_bytes=30 * 1024 * 1024),
         name="project_last",
-    )(at, *keep_far(*xs, *pieces, part), counts, *keep_far(head))
+    )(at, *keep_far(*xs), *pieces, *keep_far(part), counts, *keep_far(head))
 
 
 def normalize(pre_ref, emb_ref, inverse_ref):
@@ -631,6 +631,7 @@
     first_far, second_far = shift(first_up, 2, 1), shift(second_down, 2, -1)
     middle = [second_up, second_down]
     other_middle = [swap(piece) for piece in middle]
+    early = [keep_far(*some) for some in early]
     head, part = project_middle(at, 8, xs, early[0] + middle + early[1] + other_middle, part, head)
     first_far, second_far, part = together(first_far, second_far, part)
     late = [first_far, second_far, swap(first_far), swap(second_far)]

time: 199 us -> 196 us (0.985)
  local copies, waits for them, and re-layouts: 10.4 us -> 5.95 us
  starting transfers between devices: 48.9 us -> 51.2 us
    unnamed x19 -> x21, local copies, waits for them, and re-layouts: 6.89 us -> 4.03 us
  transfers between devices with their start and end apart: 42 -> 42, of which waited for: 21 -> 20; matrix products, arithmetic and copies ran while one was open for 6% -> 5% of each run, Pallas kernels for 33% -> 34%
where the time goes in v1:
time: 196 us; the launch traced here: 195 us
  Pallas kernels  81.3 us (41%)
  starting transfers between devices  51.2 us (26%)
  waiting for transfers between devices  48 us (24%)
  local copies, waits for them, and re-layouts  5.95 us (3%)
  matrix products  4.13 us (2%)
  other arithmetic  3.35 us (2%)
    ppermute x23, starting transfers between devices, shift(): return lax.ppermute(value, ('c', 'y', 'z'), pairs)  35.1 us
    ppermute x23, waiting for transfers between devices, shift(): return lax.ppermute(value, ('c', 'y', 'z'), pairs)  29.7 us
    pallas_call x3, Pallas kernels, input_grad(): pl.pallas_call(lambda *refs: input_grad_kernel(count, *refs), grid=(steps...  20.5 us
    pallas_call x1, Pallas kernels, project_middle(): pl.pallas_call(lambda *refs: project_middle_kernel(count, early, *refs),...  14.8 us
    pallas_call x1, Pallas kernels, project_last(): pl.pallas_call(lambda *refs: project_last_kernel(count, *refs), in_specs=...  13 us
    pallas_call x4, Pallas kernels, head_partial(): pl.pallas_call(lambda *refs: partial_kernel(outs, len(adds[0]), *refs), i...  11.6 us
    pallas_call x1, Pallas kernels, project_early(): pl.pallas_call(lambda *refs: project_early_kernel(count, *refs), in_specs...  10.2 us
    ppermute x14, waiting for transfers between devices, swap(): return lax.ppermute(value, 'c', SWAP)  7.35 us
  transfers between devices with their start and end apart: 42, of which 20 were waited for; matrix products, arithmetic and copies ran while one was open for 5% of the time, Pallas kernels for 34%

profile of v1, /device:TPU:0, one launch (start us, length us, event | category | flops | bytes accessed | tf_op | source)
XLA Modules:
  0.0 194.9 jit_solution(1829899122789119016)
XLA Ops:
  4.4 4.1 %convolution_convert_fusion = bf16[384,4096]{1,0:T(8,128)(2,1)} fusion(bf16[192,4096]{1,0:T(8,128)(2,1)} %refs_1_.6, s32[384]{0:T(512)S(1)} %eq.458), kind=kOutput, calls=%fused_computation | convolution fusion | flops 605626368 | bytes 4720128 | tf_op jit(solution)/shard_map/dot_general | solution.py:586
  14.2 4.5 %all-to-all-start = ((bf16[8,48,4096]{2,1,0:T(8,128)(2,1)}), bf16[8,48,4096]{2,1,0:T(8,128)(2,1)}, u32[]{:S(2)}, u32[]{:S(2)}) async-start(bf16[8,48,4096]{2,1,0:T(8,128)(2,1)} %bitcast.32), calls=%async_computation | async-start | bytes 6291456 | tf_op jit(solution)/shard_map/all_to_all | solution.py:604
  27.6 6.8 %collective-permute-done.2 = bf16[256,1024]{1,0:T(8,128)(2,1)S(1)} collective-permute-done((bf16[256,1024]{1,0:T(8,128)(2,1)S(1)}, bf16[256,1024]{1,0:T(8,128)(2,1)S(1)}, u32[]{:S(2)}, u32[]{:S(2)}) %collective-permute-start.2) | collective-permute-done | bytes 524320 | tf_op jit(solution)/shard_map/ppermute | solution.py:27
  37.7 3.1 %collective-permute-start.8 = (bf16[512,1024]{1,0:T(8,128)(2,1)S(1)}, bf16[512,1024]{1,0:T(8,128)(2,1)S(1)}, u32[]{:S(2)}, u32[]{:S(2)}) collective-permute-start(bf16[512,1024]{1,0:T(8,128)(2,1)S(1)} %constant_dynamic-update-slice_fusion.refs_5_.refs_6_), channel_id=1, source_target_pairs={{0,3},{1,0},{2,1},{3,2},{4,7},{5,4},{6,5},{7,6},{8,11},{9,8},{10,9... | collective-permute-start | bytes 3145736 | tf_op jit(solution)/shard_map/ppermute | solution.py:27
  43.0 10.2 %project_early.1 = (bf16[4096,2048]{1,0:T(8,128)(2,1)}, bf16[384,2048]{1,0:T(8,128)(2,1)}) custom-call(s32[2,32]{1,0:T(2,128)S(1)} %pad_add_fusion.refs_0_, bf16[192,4096]{1,0:T(8,128)(2,1)} %refs_0_, bf16[192,4096]{1,0:T(8,128)(2,1)} %refs_1_.6, bf16[256,1024]{1,0:T(8,128)(2,1)} %copy-done.4, bf16[256,1024]{1,0:T(8,128)(2,1)} %copy-done.5, ...), custom_call_target="tpu_custom_call" | custom-call | tf_op jit(solution)/shard_map/project_early/pallas_call | solution.py:180
  57.6 14.8 %project_middle.1 = (bf16[4096,2048]{1,0:T(8,128)(2,1)}, bf16[768,2048]{1,0:T(8,128)(2,1)}) custom-call(s32[2,32]{1,0:T(2,128)S(1)} %pad_add_fusion.refs_0_, bf16[192,4096]{1,0:T(8,128)(2,1)} %refs_0_, bf16[192,4096]{1,0:T(8,128)(2,1)} %refs_1_.6, bf16[384,4096]{1,0:T(8,128)(2,1)} %bitcast.33.refs_3_, ...), custom_call_target="tpu_custom_call", output_to_operand_aliasing={{0}: (21, {})} | custom-call | tf_op jit(solution)/shard_map/project_middle/pallas_call | solution.py:250
  76.9 13.0 %project_last.1 = (bf16[4096,2048]{1,0:T(8,128)(2,1)}, bf16[768,2048]{1,0:T(8,128)(2,1)}, f32[768,128]{1,0:T(8,128)}, bf16[192,384]{1,0:T(8,128)(2,1)}, f32[192,128]{1,0:T(8,128)}, /*index=5*/bf16[384,2048]{1,0:T(8,128)(2,1)}) custom-call(s32[2,32]{1,0:T(2,128)S(1)} %pad_add_fusion.refs_0_, ...), custom_call_target="tpu_custom_call", output_to_operand_aliasing={{0}: (10, {})} | custom-call | tf_op jit(solution)/shard_map/project_last/pallas_call | solution.py:316
  90.5 4.5 %all-to-all-start.1 = ((bf16[8,48,2048]{2,1,0:T(8,128)(2,1)}), bf16[8,48,2048]{2,1,0:T(8,128)(2,1)S(1)}, u32[]{:S(2)}, u32[]{:S(2)}) async-start(bf16[8,48,2048]{2,1,0:T(8,128)(2,1)} %bitcast.68), calls=%async_computation.1 | async-start | bytes 3145728 | tf_op jit(solution)/shard_map/all_to_all | solution.py:639
  95.0 3.4 %slopes_of.2 = (bf16[192,2048]{1,0:T(8,128)(2,1)S(1)}, bf16[192,1024]{1,0:T(8,128)(2,1)S(1)}, bf16[192,1024]{1,0:T(8,128)(2,1)S(1)}) custom-call(s32[2,4]{1,0:T(2,128)S(1)} %pad_add_fusion.1.refs_0_, f32[768,128]{1,0:T(8,128)} %get-tuple-element.96.refs_1_, f32[192,128]{1,0:T(8,128)} %get-tuple-element.98.refs_2_, ...), custom_call_target="tpu_custom_call" | custom-call | tf_op jit(solution)/shard_map/slopes_of/pallas_call | solution.py:441
  98.4 6.7 %input_grad.3.refs_3_ = bf16[192,4096]{1,0:T(8,128)(2,1)} custom-call(bf16[192,2048]{1,0:T(8,128)(2,1)S(1)} %get-tuple-element.101.refs_0_, bf16[4096,2048]{1,0:T(8,128)(2,1)} %get-tuple-element.102.refs_1_.refs_2_), custom_call_target="tpu_custom_call" | custom-call | flops 1 | bytes 1 | tf_op jit(solution)/shard_map/input_grad/pallas_call | solution.py:479
  105.1 4.8 %turn.1.refs_1_ = bf16[4096,768]{1,0:T(8,128)(2,1)} custom-call(bf16[192,4096]{1,0:T(8,128)(2,1)} %refs_0_, bf16[192,4096]{1,0:T(8,128)(2,1)} %refs_1_.6, bf16[192,4096]{1,0:T(8,128)(2,1)} %collective-permute-done.21.refs_2_, bf16[192,4096]{1,0:T(8,128)(2,1)} %collective-permute-done.22.refs_3_), custom_call_target="tpu_custom_call" | custom-call | flops 1 | bytes 1 | tf_op jit(solution)/shard_map/turn/pallas_call | solution.py:75
  109.9 6.6 %all-to-all-done.1 = bf16[8,48,2048]{2,1,0:T(8,128)(2,1)S(1)} async-done(((bf16[8,48,2048]{2,1,0:T(8,128)(2,1)}), bf16[8,48,2048]{2,1,0:T(8,128)(2,1)S(1)}, u32[]{:S(2)}, u32[]{:S(2)}) %all-to-all-start.1) | async-done | bytes 1572896 | tf_op jit(solution)/shard_map/all_to_all | solution.py:639
  116.5 3.1 %slopes_of.3 = (bf16[192,2048]{1,0:T(8,128)(2,1)S(1)}, bf16[192,1024]{1,0:T(8,128)(2,1)S(1)}, bf16[192,1024]{1,0:T(8,128)(2,1)S(1)}) custom-call(s32[2,4]{1,0:T(2,128)S(1)} %pad_add_fusion.1.refs_0_, f32[768,128]{1,0:T(8,128)} %get-tuple-element.96.refs_1_, f32[192,128]{1,0:T(8,128)} %get-tuple-element.98.refs_2_, ...), custom_call_target="tpu_custom_call" | custom-call | tf_op jit(solution)/shard_map/slopes_of/pallas_call | solution.py:441
  124.8 2.9 %collective-permute-start.26 = (bf16[512,1024]{1,0:T(8,128)(2,1)S(1)}, bf16[512,1024]{1,0:T(8,128)(2,1)S(1)}, u32[]{:S(2)}, u32[]{:S(2)}) collective-permute-start(bf16[512,1024]{1,0:T(8,128)(2,1)S(1)} %get-tuple-element.114), channel_id=1, source_target_pairs={{0,12},{1,13},{2,14},{3,15},{4,0},{5,1},{6,2},{7,3},{8,4},{9,5},{1... | collective-permute-start | bytes 3145736 | tf_op jit(solution)/shard_map/ppermute | solution.py:27
  132.9 6.7 %input_grad.4.refs_4_ = bf16[192,4096]{1,0:T(8,128)(2,1)} custom-call(bf16[192,2048]{1,0:T(8,128)(2,1)S(1)} %get-tuple-element.129.refs_0_.refs_1_, bf16[4096,2048]{1,0:T(8,128)(2,1)} %get-tuple-element.102.refs_1_.refs_2_), custom_call_target="tpu_custom_call" | custom-call | flops 1 | bytes 1 | tf_op jit(solution)/shard_map/input_grad/pallas_call | solution.py:479
  140.6 2.9 %head_partial.6 = (bf16[512,1024]{1,0:T(8,128)(2,1)S(1)}, bf16[512,1024]{1,0:T(8,128)(2,1)S(1)}) custom-call(s32[4]{0:T(128)S(1)} %pad_add_fusion.2.refs_0_, bf16[4096,768]{1,0:T(8,128)(2,1)S(1)} %copy-done.2, bf16[768,1024]{1,0:T(8,128)(2,1)S(1)} %constant_dynamic-update-slice_fusion.4.refs_2_, bf16[512,1024]{1,0:T(8,128)(2,1)S(1)} %collective-permute-done.25.refs_3_, ...), custom_call_target="tpu_custom_call" | custom-call | tf_op jit(solution)/shard_map/head_partial/pallas_call | solution.py:513
  146.9 4.4 %collective-permute-done.29.refs_3_ = bf16[512,1024]{1,0:T(8,128)(2,1)S(1)} collective-permute-done((bf16[512,1024]{1,0:T(8,128)(2,1)S(1)}, bf16[512,1024]{1,0:T(8,128)(2,1)S(1)}, u32[]{:S(2)}, u32[]{:S(2)}) %collective-permute-start.29) | collective-permute-done | bytes 1048608 | tf_op jit(solution)/shard_map/ppermute | solution.py:27
  154.7 7.2 %input_grad.5 = (bf16[192,4096]{1,0:T(8,128)(2,1)}, bf16[192,4096]{1,0:T(8,128)(2,1)}) custom-call(bf16[192,2048]{1,0:T(8,128)(2,1)S(1)} %get-tuple-element.101.refs_0_, bf16[192,2048]{1,0:T(8,128)(2,1)S(1)} %get-tuple-element.129.refs_0_.refs_1_, ...), custom_call_target="tpu_custom_call", output_to_operand_aliasing={{0}: (3, {}), {1}: (4, {})} | custom-call | flops 1 | bytes 1 | tf_op jit(solution)/shard_map/input_grad/pallas_call | solution.py:479
  163.1 3.5 %collective-permute-start.34 = (bf16[128,1024]{1,0:T(8,128)(2,1)S(1)}, bf16[128,1024]{1,0:T(8,128)(2,1)S(1)}, u32[]{:S(2)}, u32[]{:S(2)}) collective-permute-start(bf16[128,1024]{1,0:T(8,128)(2,1)S(1)} %add_convert_fusion.4), channel_id=1, source_target_pairs={{0,3},{1,0},{2,1},{3,2},{4,7},{5,4},{6,5},{7,6},{8,11},{9,8},{10,9... | collective-permute-start | bytes 786440 | tf_op jit(solution)/shard_map/ppermute | solution.py:27
  167.0 3.2 %collective-permute-start.32 = (bf16[128,1024]{1,0:T(8,128)(2,1)S(1)}, bf16[128,1024]{1,0:T(8,128)(2,1)S(1)}, u32[]{:S(2)}, u32[]{:S(2)}) collective-permute-start(bf16[128,1024]{1,0:T(8,128)(2,1)S(1)} %get-tuple-element.152), channel_id=1, source_target_pairs={{0,3},{1,0},{2,1},{3,2},{4,7},{5,4},{6,5},{7,6},{8,11},{9,8},{10,9... | collective-permute-start | bytes 786440 | tf_op jit(solution)/shard_map/ppermute | solution.py:27
  170.5 4.0 %collective-permute-done.31 = bf16[128,1024]{1,0:T(8,128)(2,1)S(1)} collective-permute-done((bf16[128,1024]{1,0:T(8,128)(2,1)S(1)}, bf16[128,1024]{1,0:T(8,128)(2,1)S(1)}, u32[]{:S(2)}, u32[]{:S(2)}) %collective-permute-start.31) | collective-permute-done | bytes 262176 | tf_op jit(solution)/shard_map/ppermute | solution.py:27
  174.6 3.2 %collective-permute-done.33 = bf16[128,1024]{1,0:T(8,128)(2,1)S(1)} collective-permute-done((bf16[128,1024]{1,0:T(8,128)(2,1)S(1)}, bf16[128,1024]{1,0:T(8,128)(2,1)S(1)}, u32[]{:S(2)}, u32[]{:S(2)}) %collective-permute-start.33) | collective-permute-done | bytes 262176 | tf_op jit(solution)/shard_map/ppermute | solution.py:27
  180.2 4.1 %collective-permute-done.36 = bf16[128,1024]{1,0:T(8,128)(2,1)S(1)} collective-permute-done((bf16[128,1024]{1,0:T(8,128)(2,1)S(1)}, bf16[128,1024]{1,0:T(8,128)(2,1)S(1)}, u32[]{:S(2)}, u32[]{:S(2)}) %collective-permute-start.36) | collective-permute-done | bytes 262176 | tf_op jit(solution)/shard_map/ppermute | solution.py:27
  189.9 3.0 %collective-permute-done.37 = bf16[256,256]{1,0:T(8,128)(2,1)S(1)} collective-permute-done((bf16[256,256]{1,0:T(8,128)(2,1)S(1)}, bf16[256,256]{1,0:T(8,128)(2,1)S(1)}, u32[]{:S(2)}, u32[]{:S(2)}) %collective-permute-start.37) | collective-permute-done | bytes 131104 | tf_op jit(solution)/shard_map/ppermute | solution.py:571
  (119 shorter events, 63.3 us)
Async XLA Ops:
  1.9 16.8 %collective-permute-start.1 = (bf16[256,1024]{1,0:T(8,128)(2,1)S(1)}, bf16[256,1024]{1,0:T(8,128)(2,1)S(1)}, u32[]{:S(2)}, u32[]{:S(2)}) collective-permute-start(bf16[256,1024]{1,0:T(8,128)(2,1)S(1)} %constant_dynamic-slice_fusion.refs_3_.refs_4_), channel_id=1, source_target_pairs={{0,4},{1,5},{2,6},{3,7},{4,8},{5,9},{6,10},{7,11},{8,12},{9,13},{1... | collective-permute-start | bytes 1572872 | tf_op jit(solution)/shard_map/ppermute | solution.py:27
  8.5 11.2 %collective-permute-start.5 = (bf16[256,1024]{1,0:T(8,128)(2,1)S(1)}, bf16[256,1024]{1,0:T(8,128)(2,1)S(1)}, u32[]{:S(2)}, u32[]{:S(2)}) collective-permute-start(bf16[256,1024]{1,0:T(8,128)(2,1)S(1)} %constant_dynamic-slice_fusion.refs_3_.refs_4_), channel_id=1, source_target_pairs={{0,1},{1,2},{2,3},{3,0},{4,5},{5,6},{6,7},{7,4},{8,9},{9,10},{10,1... | collective-permute-start | bytes 1572872 | tf_op jit(solution)/shard_map/ppermute | solution.py:27
  10.5 14.8 %collective-permute-start.6 = (bf16[256,1024]{1,0:T(8,128)(2,1)S(1)}, bf16[256,1024]{1,0:T(8,128)(2,1)}, u32[]{:S(2)}, u32[]{:S(2)}) collective-permute-start(bf16[256,1024]{1,0:T(8,128)(2,1)S(1)} %constant_dynamic-slice_fusion.refs_3_.refs_4_), channel_id=1, source_target_pairs={{0,3},{1,0},{2,1},{3,2},{4,7},{5,4},{6,5},{7,6},{8,11},{9,8},{10,9... | collective-permute-start | bytes 1572872 | tf_op jit(solution)/shard_map/ppermute | solution.py:27
  12.6 12.7 %collective-permute-start = (bf16[256,1024]{1,0:T(8,128)(2,1)S(1)}, bf16[256,1024]{1,0:T(8,128)(2,1)}, u32[]{:S(2)}, u32[]{:S(2)}) collective-permute-start(bf16[256,1024]{1,0:T(8,128)(2,1)S(1)} %constant_dynamic-slice_fusion.refs_3_.refs_4_), channel_id=1, source_target_pairs={{0,12},{1,13},{2,14},{3,15},{4,0},{5,1},{6,2},{7,3},{8,4},{9,5},{1... | collective-permute-start | bytes 1572872 | tf_op jit(solution)/shard_map/ppermute | solution.py:27
  14.2 43.0 %all-to-all-start = ((bf16[8,48,4096]{2,1,0:T(8,128)(2,1)}), bf16[8,48,4096]{2,1,0:T(8,128)(2,1)}, u32[]{:S(2)}, u32[]{:S(2)}) async-start(bf16[8,48,4096]{2,1,0:T(8,128)(2,1)} %bitcast.32), calls=%async_computation | async-start | bytes 6291456 | tf_op jit(solution)/shard_map/all_to_all | solution.py:604
  18.8 15.6 %collective-permute-start.2 = (bf16[256,1024]{1,0:T(8,128)(2,1)S(1)}, bf16[256,1024]{1,0:T(8,128)(2,1)S(1)}, u32[]{:S(2)}, u32[]{:S(2)}) collective-permute-start(bf16[256,1024]{1,0:T(8,128)(2,1)S(1)} %collective-permute-done.1.refs_4_.refs_5_), channel_id=1, source_target_pairs={{0,4},{1,5},{2,6},{3,7},{4,8},{5,9},{6,10},{7,11},{8,12},{9,13},{1... | collective-permute-start | bytes 1572872 | tf_op jit(solution)/shard_map/ppermute | solution.py:27
  19.2 15.1 %collective-permute-start.3 = (bf16[256,1024]{1,0:T(8,128)(2,1)S(1)}, bf16[256,1024]{1,0:T(8,128)(2,1)S(1)}, u32[]{:S(2)}, u32[]{:S(2)}) collective-permute-start(bf16[256,1024]{1,0:T(8,128)(2,1)S(1)} %collective-permute-done.1.refs_4_.refs_5_), channel_id=1, source_target_pairs={{0,1},{1,2},{2,3},{3,0},{4,5},{5,6},{6,7},{7,4},{8,9},{9,10},{10,1... | collective-permute-start | bytes 1572872 | tf_op jit(solution)/shard_map/ppermute | solution.py:27
  19.7 14.6 %collective-permute-start.4 = (bf16[256,1024]{1,0:T(8,128)(2,1)S(1)}, bf16[256,1024]{1,0:T(8,128)(2,1)}, u32[]{:S(2)}, u32[]{:S(2)}) collective-permute-start(bf16[256,1024]{1,0:T(8,128)(2,1)S(1)} %collective-permute-done.1.refs_4_.refs_5_), channel_id=1, source_target_pairs={{0,3},{1,0},{2,1},{3,2},{4,7},{5,4},{6,5},{7,6},{8,11},{9,8},{10,9... | collective-permute-start | bytes 1572872 | tf_op jit(solution)/shard_map/ppermute | solution.py:27
  25.3 11.4 %collective-permute-start.9 = (bf16[256,1024]{1,0:T(8,128)(2,1)S(1)}, bf16[256,1024]{1,0:T(8,128)(2,1)}, u32[]{:S(2)}, u32[]{:S(2)}) collective-permute-start(bf16[256,1024]{1,0:T(8,128)(2,1)S(1)} %constant_dynamic-slice_fusion.refs_3_.refs_4_), channel_id=1, source_target_pairs={{0,16},{16,0},{1,17},{17,1},{2,18},{18,2},{3,19},{19,3},{4,20},{20... | collective-permute-start | bytes 1572872 | tf_op jit(solution)/shard_map/ppermute | solution.py:31
  25.3 11.6 %collective-permute-start.10 = (bf16[256,1024]{1,0:T(8,128)(2,1)S(1)}, bf16[256,1024]{1,0:T(8,128)(2,1)S(1)}, u32[]{:S(2)}, u32[]{:S(2)}) collective-permute-start(bf16[256,1024]{1,0:T(8,128)(2,1)S(1)} %collective-permute-done.1.refs_4_.refs_5_), channel_id=1, source_target_pairs={{0,16},{16,0},{1,17},{17,1},{2,18},{18,2},{3,19},{19,3},{4,20},{20... | collective-permute-start | bytes 1572872 | tf_op jit(solution)/shard_map/ppermute | solution.py:31
  36.6 16.6 %collective-permute-start.7 = (bf16[512,1024]{1,0:T(8,128)(2,1)S(1)}, bf16[512,1024]{1,0:T(8,128)(2,1)S(1)}, u32[]{:S(2)}, u32[]{:S(2)}) collective-permute-start(bf16[512,1024]{1,0:T(8,128)(2,1)S(1)} %constant_dynamic-update-slice_fusion.refs_5_.refs_6_), channel_id=1, source_target_pairs={{0,1},{1,2},{2,3},{3,0},{4,5},{5,6},{6,7},{7,4},{8,9},{9,10},{10,1... | collective-permute-start | bytes 3145736 | tf_op jit(solution)/shard_map/ppermute | solution.py:27
  37.7 15.5 %collective-permute-start.8 = (bf16[512,1024]{1,0:T(8,128)(2,1)S(1)}, bf16[512,1024]{1,0:T(8,128)(2,1)S(1)}, u32[]{:S(2)}, u32[]{:S(2)}) collective-permute-start(bf16[512,1024]{1,0:T(8,128)(2,1)S(1)} %constant_dynamic-update-slice_fusion.refs_5_.refs_6_), channel_id=1, source_target_pairs={{0,3},{1,0},{2,1},{3,2},{4,7},{5,4},{6,5},{7,6},{8,11},{9,8},{10,9... | collective-permute-start | bytes 3145736 | tf_op jit(solution)/shard_map/ppermute | solution.py:27
  53.8 18.6 %collective-permute-start.15 = (bf16[512,1024]{1,0:T(8,128)(2,1)}, bf16[512,1024]{1,0:T(8,128)(2,1)}, u32[]{:S(2)}, u32[]{:S(2)}) collective-permute-start(bf16[512,1024]{1,0:T(8,128)(2,1)} %constant_dynamic-update-slice_fusion.2.refs_6_.refs_7_), channel_id=1, source_target_pairs={{0,1},{1,2},{2,3},{3,0},{4,5},{5,6},{6,7},{7,4},{8,9},{9,10},{10,1... | collective-permute-start | bytes 3145736 | tf_op jit(solution)/shard_map/ppermute | solution.py:27
  54.9 17.5 %collective-permute-start.16 = (bf16[512,1024]{1,0:T(8,128)(2,1)S(1)}, bf16[512,1024]{1,0:T(8,128)(2,1)}, u32[]{:S(2)}, u32[]{:S(2)}) collective-permute-start(bf16[512,1024]{1,0:T(8,128)(2,1)S(1)} %collective-permute-done.8.refs_11_), channel_id=1, source_target_pairs={{0,3},{1,0},{2,1},{3,2},{4,7},{5,4},{6,5},{7,6},{8,11},{9,8},{10,9... | collective-permute-start | bytes 3145736 | tf_op jit(solution)/shard_map/ppermute | solution.py:27
  89.9 15.2 %collective-permute-start.21 = (bf16[192,4096]{1,0:T(8,128)(2,1)}, bf16[192,4096]{1,0:T(8,128)(2,1)}, u32[]{:S(2)}, u32[]{:S(2)}) collective-permute-start(bf16[192,4096]{1,0:T(8,128)(2,1)} %refs_0_), channel_id=1, source_target_pairs={{0,16},{16,0},{1,17},{17,1},{2,18},{18,2},{3,19},{19,3},{4,20},{20... | collective-permute-start | bytes 4718600 | tf_op jit(solution)/shard_map/ppermute | solution.py:31
  90.1 15.0 %collective-permute-start.22 = (bf16[192,4096]{1,0:T(8,128)(2,1)}, bf16[192,4096]{1,0:T(8,128)(2,1)}, u32[]{:S(2)}, u32[]{:S(2)}) collective-permute-start(bf16[192,4096]{1,0:T(8,128)(2,1)} %refs_1_.6), channel_id=1, source_target_pairs={{0,16},{16,0},{1,17},{17,1},{2,18},{18,2},{3,19},{19,3},{4,20},{20... | collective-permute-start | bytes 4718600 | tf_op jit(solution)/shard_map/ppermute | solution.py:31
  90.5 26.0 %all-to-all-start.1 = ((bf16[8,48,2048]{2,1,0:T(8,128)(2,1)}), bf16[8,48,2048]{2,1,0:T(8,128)(2,1)S(1)}, u32[]{:S(2)}, u32[]{:S(2)}) async-start(bf16[8,48,2048]{2,1,0:T(8,128)(2,1)} %bitcast.68), calls=%async_computation.1 | async-start | bytes 3145728 | tf_op jit(solution)/shard_map/all_to_all | solution.py:639
  124.5 16.1 %collective-permute-start.25 = (bf16[512,1024]{1,0:T(8,128)(2,1)S(1)}, bf16[512,1024]{1,0:T(8,128)(2,1)S(1)}, u32[]{:S(2)}, u32[]{:S(2)}) collective-permute-start(bf16[512,1024]{1,0:T(8,128)(2,1)S(1)} %get-tuple-element.113), channel_id=1, source_target_pairs={{0,4},{1,5},{2,6},{3,7},{4,8},{5,9},{6,10},{7,11},{8,12},{9,13},{1... | collective-permute-start | bytes 3145736 | tf_op jit(solution)/shard_map/ppermute | solution.py:27
  124.8 15.7 %collective-permute-start.26 = (bf16[512,1024]{1,0:T(8,128)(2,1)S(1)}, bf16[512,1024]{1,0:T(8,128)(2,1)S(1)}, u32[]{:S(2)}, u32[]{:S(2)}) collective-permute-start(bf16[512,1024]{1,0:T(8,128)(2,1)S(1)} %get-tuple-element.114), channel_id=1, source_target_pairs={{0,12},{1,13},{2,14},{3,15},{4,0},{5,1},{6,2},{7,3},{8,4},{9,5},{1... | collective-permute-start | bytes 3145736 | tf_op jit(solution)/shard_map/ppermute | solution.py:27
  130.8 20.5 %collective-permute-start.29 = (bf16[512,1024]{1,0:T(8,128)(2,1)S(1)}, bf16[512,1024]{1,0:T(8,128)(2,1)S(1)}, u32[]{:S(2)}, u32[]{:S(2)}) collective-permute-start(bf16[512,1024]{1,0:T(8,128)(2,1)S(1)} %get-tuple-element.123), channel_id=1, source_target_pairs={{0,12},{1,13},{2,14},{3,15},{4,0},{5,1},{6,2},{7,3},{8,4},{9,5},{1... | collective-permute-start | bytes 3145736 | tf_op jit(solution)/shard_map/ppermute | solution.py:27
  132.0 19.7 %collective-permute-start.30 = (bf16[512,1024]{1,0:T(8,128)(2,1)S(1)}, bf16[512,1024]{1,0:T(8,128)(2,1)S(1)}, u32[]{:S(2)}, u32[]{:S(2)}) collective-permute-start(bf16[512,1024]{1,0:T(8,128)(2,1)S(1)} %get-tuple-element.124), channel_id=1, source_target_pairs={{0,4},{1,5},{2,6},{3,7},{4,8},{5,9},{6,10},{7,11},{8,12},{9,13},{1... | collective-permute-start | bytes 3145736 | tf_op jit(solution)/shard_map/ppermute | solution.py:27
  143.5 19.6 %collective-permute-start.27 = (bf16[512,1024]{1,0:T(8,128)(2,1)S(1)}, bf16[512,1024]{1,0:T(8,128)(2,1)S(1)}, u32[]{:S(2)}, u32[]{:S(2)}) collective-permute-start(bf16[512,1024]{1,0:T(8,128)(2,1)S(1)} %get-tuple-element.121), channel_id=1, source_target_pairs={{0,4},{1,5},{2,6},{3,7},{4,8},{5,9},{6,10},{7,11},{8,12},{9,13},{1... | collective-permute-start | bytes 3145736 | tf_op jit(solution)/shard_map/ppermute | solution.py:27
  144.2 18.8 %collective-permute-start.28 = (bf16[512,1024]{1,0:T(8,128)(2,1)S(1)}, bf16[512,1024]{1,0:T(8,128)(2,1)S(1)}, u32[]{:S(2)}, u32[]{:S(2)}) collective-permute-start(bf16[512,1024]{1,0:T(8,128)(2,1)S(1)} %get-tuple-element.122), channel_id=1, source_target_pairs={{0,12},{1,13},{2,14},{3,15},{4,0},{5,1},{6,2},{7,3},{8,4},{9,5},{1... | collective-permute-start | bytes 3145736 | tf_op jit(solution)/shard_map/ppermute | solution.py:27
  166.9 7.7 %collective-permute-start.31 = (bf16[128,1024]{1,0:T(8,128)(2,1)S(1)}, bf16[128,1024]{1,0:T(8,128)(2,1)S(1)}, u32[]{:S(2)}, u32[]{:S(2)}) collective-permute-start(bf16[128,1024]{1,0:T(8,128)(2,1)S(1)} %get-tuple-element.153), channel_id=1, source_target_pairs={{0,1},{1,2},{2,3},{3,0},{4,5},{5,6},{6,7},{7,4},{8,9},{9,10},{10,1... | collective-permute-start | bytes 786440 | tf_op jit(solution)/shard_map/ppermute | solution.py:27
  (26 other events, 171.8 us)

commit v2 on v1

--- a/solution.py
+++ b/solution.py
@@ -505,7 +505,7 @@
             refs[outs * adds + i][part, :] = total.astype(BF16)
             return 0
 
-        lax.fori_loop(0, 2, block, 0)
+        lax.fori_loop(0, 2, block, 0, unroll=adds == 0)
 
 
 def head_partial(states, slopes, at, adds):

time: 196 us -> 195 us (level)
  transfers between devices with their start and end apart: 42 -> 42, of which waited for: 20 -> 20; matrix products, arithmetic and copies ran while one was open for 5% -> 5% of each run, Pallas kernels for 34% -> 33%
where the time goes in v2:
time: 195 us; the launch traced here: 194 us
  Pallas kernels  80.3 us (41%)
  starting transfers between devices  51.2 us (26%)
  waiting for transfers between devices  48.5 us (25%)
  local copies, waits for them, and re-layouts  5.95 us (3%)
  matrix products  4.13 us (2%)
  other arithmetic  3.35 us (2%)
    ppermute x23, starting transfers between devices, shift(): return lax.ppermute(value, ('c', 'y', 'z'), pairs)  35.1 us
    ppermute x23, waiting for transfers between devices, shift(): return lax.ppermute(value, ('c', 'y', 'z'), pairs)  30.3 us
    pallas_call x3, Pallas kernels, input_grad(): pl.pallas_call(lambda *refs: input_grad_kernel(count, *refs), grid=(steps...  20.5 us
    pallas_call x1, Pallas kernels, project_middle(): pl.pallas_call(lambda *refs: project_middle_kernel(count, early, *refs),...  14.8 us
    pallas_call x1, Pallas kernels, project_last(): pl.pallas_call(lambda *refs: project_last_kernel(count, *refs), in_specs=...  13 us
    pallas_call x4, Pallas kernels, head_partial(): pl.pallas_call(lambda *refs: partial_kernel(outs, len(adds[0]), *refs), i...  10.5 us
    pallas_call x1, Pallas kernels, project_early(): pl.pallas_call(lambda *refs: project_early_kernel(count, *refs), in_specs...  10.2 us
    ppermute x14, waiting for transfers between devices, swap(): return lax.ppermute(value, 'c', SWAP)  7.35 us
  transfers between devices with their start and end apart: 42, of which 20 were waited for; matrix products, arithmetic and copies ran while one was open for 5% of the time, Pallas kernels for 33%

profile of v2, /device:TPU:0, one launch (start us, length us, event | category | flops | bytes accessed | tf_op | source)
XLA Modules:
  0.0 194.4 jit_solution(1929899775380652160)
XLA Ops:
  4.4 4.1 %convolution_convert_fusion = bf16[384,4096]{1,0:T(8,128)(2,1)} fusion(bf16[192,4096]{1,0:T(8,128)(2,1)} %refs_1_.6, s32[384]{0:T(512)S(1)} %eq.458), kind=kOutput, calls=%fused_computation | convolution fusion | flops 605626368 | bytes 4720128 | tf_op jit(solution)/shard_map/dot_general | solution.py:586
  14.2 4.5 %all-to-all-start = ((bf16[8,48,4096]{2,1,0:T(8,128)(2,1)}), bf16[8,48,4096]{2,1,0:T(8,128)(2,1)}, u32[]{:S(2)}, u32[]{:S(2)}) async-start(bf16[8,48,4096]{2,1,0:T(8,128)(2,1)} %bitcast.32), calls=%async_computation | async-start | bytes 6291456 | tf_op jit(solution)/shard_map/all_to_all | solution.py:604
  27.6 6.8 %collective-permute-done.2 = bf16[256,1024]{1,0:T(8,128)(2,1)S(1)} collective-permute-done((bf16[256,1024]{1,0:T(8,128)(2,1)S(1)}, bf16[256,1024]{1,0:T(8,128)(2,1)S(1)}, u32[]{:S(2)}, u32[]{:S(2)}) %collective-permute-start.2) | collective-permute-done | bytes 524320 | tf_op jit(solution)/shard_map/ppermute | solution.py:27
  37.7 3.1 %collective-permute-start.8 = (bf16[512,1024]{1,0:T(8,128)(2,1)S(1)}, bf16[512,1024]{1,0:T(8,128)(2,1)S(1)}, u32[]{:S(2)}, u32[]{:S(2)}) collective-permute-start(bf16[512,1024]{1,0:T(8,128)(2,1)S(1)} %constant_dynamic-update-slice_fusion.refs_5_.refs_6_), channel_id=1, source_target_pairs={{0,3},{1,0},{2,1},{3,2},{4,7},{5,4},{6,5},{7,6},{8,11},{9,8},{10,9... | collective-permute-start | bytes 3145736 | tf_op jit(solution)/shard_map/ppermute | solution.py:27
  43.0 10.2 %project_early.1 = (bf16[4096,2048]{1,0:T(8,128)(2,1)}, bf16[384,2048]{1,0:T(8,128)(2,1)}) custom-call(s32[2,32]{1,0:T(2,128)S(1)} %pad_add_fusion.refs_0_, bf16[192,4096]{1,0:T(8,128)(2,1)} %refs_0_, bf16[192,4096]{1,0:T(8,128)(2,1)} %refs_1_.6, bf16[256,1024]{1,0:T(8,128)(2,1)} %copy-done.4, bf16[256,1024]{1,0:T(8,128)(2,1)} %copy-done.5, ...), custom_call_target="tpu_custom_call" | custom-call | tf_op jit(solution)/shard_map/project_early/pallas_call | solution.py:180
  57.6 14.8 %project_middle.1 = (bf16[4096,2048]{1,0:T(8,128)(2,1)}, bf16[768,2048]{1,0:T(8,128)(2,1)}) custom-call(s32[2,32]{1,0:T(2,128)S(1)} %pad_add_fusion.refs_0_, bf16[192,4096]{1,0:T(8,128)(2,1)} %refs_0_, bf16[192,4096]{1,0:T(8,128)(2,1)} %refs_1_.6, bf16[384,4096]{1,0:T(8,128)(2,1)} %bitcast.33.refs_3_, ...), custom_call_target="tpu_custom_call", output_to_operand_aliasing={{0}: (21, {})} | custom-call | tf_op jit(solution)/shard_map/project_middle/pallas_call | solution.py:250
  76.9 13.0 %project_last.1 = (bf16[4096,2048]{1,0:T(8,128)(2,1)}, bf16[768,2048]{1,0:T(8,128)(2,1)}, f32[768,128]{1,0:T(8,128)}, bf16[192,384]{1,0:T(8,128)(2,1)}, f32[192,128]{1,0:T(8,128)}, /*index=5*/bf16[384,2048]{1,0:T(8,128)(2,1)}) custom-call(s32[2,32]{1,0:T(2,128)S(1)} %pad_add_fusion.refs_0_, ...), custom_call_target="tpu_custom_call", output_to_operand_aliasing={{0}: (10, {})} | custom-call | tf_op jit(solution)/shard_map/project_last/pallas_call | solution.py:316
  90.5 4.5 %all-to-all-start.1 = ((bf16[8,48,2048]{2,1,0:T(8,128)(2,1)}), bf16[8,48,2048]{2,1,0:T(8,128)(2,1)S(1)}, u32[]{:S(2)}, u32[]{:S(2)}) async-start(bf16[8,48,2048]{2,1,0:T(8,128)(2,1)} %bitcast.68), calls=%async_computation.1 | async-start | bytes 3145728 | tf_op jit(solution)/shard_map/all_to_all | solution.py:639
  95.0 3.4 %slopes_of.2 = (bf16[192,2048]{1,0:T(8,128)(2,1)S(1)}, bf16[192,1024]{1,0:T(8,128)(2,1)S(1)}, bf16[192,1024]{1,0:T(8,128)(2,1)S(1)}) custom-call(s32[2,4]{1,0:T(2,128)S(1)} %pad_add_fusion.1.refs_0_, f32[768,128]{1,0:T(8,128)} %get-tuple-element.96.refs_1_, f32[192,128]{1,0:T(8,128)} %get-tuple-element.98.refs_2_, ...), custom_call_target="tpu_custom_call" | custom-call | tf_op jit(solution)/shard_map/slopes_of/pallas_call | solution.py:441
  98.4 6.7 %input_grad.3.refs_3_ = bf16[192,4096]{1,0:T(8,128)(2,1)} custom-call(bf16[192,2048]{1,0:T(8,128)(2,1)S(1)} %get-tuple-element.101.refs_0_, bf16[4096,2048]{1,0:T(8,128)(2,1)} %get-tuple-element.102.refs_1_.refs_2_), custom_call_target="tpu_custom_call" | custom-call | flops 1 | bytes 1 | tf_op jit(solution)/shard_map/input_grad/pallas_call | solution.py:479
  105.1 4.8 %turn.1.refs_1_ = bf16[4096,768]{1,0:T(8,128)(2,1)} custom-call(bf16[192,4096]{1,0:T(8,128)(2,1)} %refs_0_, bf16[192,4096]{1,0:T(8,128)(2,1)} %refs_1_.6, bf16[192,4096]{1,0:T(8,128)(2,1)} %collective-permute-done.21.refs_2_, bf16[192,4096]{1,0:T(8,128)(2,1)} %collective-permute-done.22.refs_3_), custom_call_target="tpu_custom_call" | custom-call | flops 1 | bytes 1 | tf_op jit(solution)/shard_map/turn/pallas_call | solution.py:75
  109.9 6.6 %all-to-all-done.1 = bf16[8,48,2048]{2,1,0:T(8,128)(2,1)S(1)} async-done(((bf16[8,48,2048]{2,1,0:T(8,128)(2,1)}), bf16[8,48,2048]{2,1,0:T(8,128)(2,1)S(1)}, u32[]{:S(2)}, u32[]{:S(2)}) %all-to-all-start.1) | async-done | bytes 1572896 | tf_op jit(solution)/shard_map/all_to_all | solution.py:639
  116.5 3.1 %slopes_of.3 = (bf16[192,2048]{1,0:T(8,128)(2,1)S(1)}, bf16[192,1024]{1,0:T(8,128)(2,1)S(1)}, bf16[192,1024]{1,0:T(8,128)(2,1)S(1)}) custom-call(s32[2,4]{1,0:T(2,128)S(1)} %pad_add_fusion.1.refs_0_, f32[768,128]{1,0:T(8,128)} %get-tuple-element.96.refs_1_, f32[192,128]{1,0:T(8,128)} %get-tuple-element.98.refs_2_, ...), custom_call_target="tpu_custom_call" | custom-call | tf_op jit(solution)/shard_map/slopes_of/pallas_call | solution.py:441
  124.3 2.9 %collective-permute-start.26 = (bf16[512,1024]{1,0:T(8,128)(2,1)S(1)}, bf16[512,1024]{1,0:T(8,128)(2,1)S(1)}, u32[]{:S(2)}, u32[]{:S(2)}) collective-permute-start(bf16[512,1024]{1,0:T(8,128)(2,1)S(1)} %get-tuple-element.114), channel_id=1, source_target_pairs={{0,12},{1,13},{2,14},{3,15},{4,0},{5,1},{6,2},{7,3},{8,4},{9,5},{1... | collective-permute-start | bytes 3145736 | tf_op jit(solution)/shard_map/ppermute | solution.py:27
  131.9 6.7 %input_grad.4.refs_4_ = bf16[192,4096]{1,0:T(8,128)(2,1)} custom-call(bf16[192,2048]{1,0:T(8,128)(2,1)S(1)} %get-tuple-element.129.refs_0_.refs_1_, bf16[4096,2048]{1,0:T(8,128)(2,1)} %get-tuple-element.102.refs_1_.refs_2_), custom_call_target="tpu_custom_call" | custom-call | flops 1 | bytes 1 | tf_op jit(solution)/shard_map/input_grad/pallas_call | solution.py:479
  146.4 4.4 %collective-permute-done.29.refs_3_ = bf16[512,1024]{1,0:T(8,128)(2,1)S(1)} collective-permute-done((bf16[512,1024]{1,0:T(8,128)(2,1)S(1)}, bf16[512,1024]{1,0:T(8,128)(2,1)S(1)}, u32[]{:S(2)}, u32[]{:S(2)}) %collective-permute-start.29) | collective-permute-done | bytes 1048608 | tf_op jit(solution)/shard_map/ppermute | solution.py:27
  151.3 2.9 %head_partial.7 = (bf16[512,1024]{1,0:T(8,128)(2,1)S(1)}, bf16[512,1024]{1,0:T(8,128)(2,1)S(1)}) custom-call(s32[4]{0:T(128)S(1)} %pad_add_fusion.5.refs_0_, bf16[4096,768]{1,0:T(8,128)(2,1)S(1)} %copy-done.2, bf16[768,1024]{1,0:T(8,128)(2,1)S(1)} %constant_dynamic-update-slice_fusion.4.refs_2_, bf16[512,1024]{1,0:T(8,128)(2,1)S(1)} %collective-permute-done.29.refs_3_, ...), custom_call_target="tpu_custom_call" | custom-call | tf_op jit(solution)/shard_map/head_partial/pallas_call | solution.py:513
  154.2 7.2 %input_grad.5 = (bf16[192,4096]{1,0:T(8,128)(2,1)}, bf16[192,4096]{1,0:T(8,128)(2,1)}) custom-call(bf16[192,2048]{1,0:T(8,128)(2,1)S(1)} %get-tuple-element.101.refs_0_, bf16[192,2048]{1,0:T(8,128)(2,1)S(1)} %get-tuple-element.129.refs_0_.refs_1_, ...), custom_call_target="tpu_custom_call", output_to_operand_aliasing={{0}: (3, {}), {1}: (4, {})} | custom-call | flops 1 | bytes 1 | tf_op jit(solution)/shard_map/input_grad/pallas_call | solution.py:479
  162.6 3.5 %collective-permute-start.34 = (bf16[128,1024]{1,0:T(8,128)(2,1)S(1)}, bf16[128,1024]{1,0:T(8,128)(2,1)S(1)}, u32[]{:S(2)}, u32[]{:S(2)}) collective-permute-start(bf16[128,1024]{1,0:T(8,128)(2,1)S(1)} %add_convert_fusion.4), channel_id=1, source_target_pairs={{0,3},{1,0},{2,1},{3,2},{4,7},{5,4},{6,5},{7,6},{8,11},{9,8},{10,9... | collective-permute-start | bytes 786440 | tf_op jit(solution)/shard_map/ppermute | solution.py:27
  166.5 3.2 %collective-permute-start.32 = (bf16[128,1024]{1,0:T(8,128)(2,1)S(1)}, bf16[128,1024]{1,0:T(8,128)(2,1)S(1)}, u32[]{:S(2)}, u32[]{:S(2)}) collective-permute-start(bf16[128,1024]{1,0:T(8,128)(2,1)S(1)} %get-tuple-element.152), channel_id=1, source_target_pairs={{0,3},{1,0},{2,1},{3,2},{4,7},{5,4},{6,5},{7,6},{8,11},{9,8},{10,9... | collective-permute-start | bytes 786440 | tf_op jit(solution)/shard_map/ppermute | solution.py:27
  170.0 4.0 %collective-permute-done.31 = bf16[128,1024]{1,0:T(8,128)(2,1)S(1)} collective-permute-done((bf16[128,1024]{1,0:T(8,128)(2,1)S(1)}, bf16[128,1024]{1,0:T(8,128)(2,1)S(1)}, u32[]{:S(2)}, u32[]{:S(2)}) %collective-permute-start.31) | collective-permute-done | bytes 262176 | tf_op jit(solution)/shard_map/ppermute | solution.py:27
  174.0 3.2 %collective-permute-done.33 = bf16[128,1024]{1,0:T(8,128)(2,1)S(1)} collective-permute-done((bf16[128,1024]{1,0:T(8,128)(2,1)S(1)}, bf16[128,1024]{1,0:T(8,128)(2,1)S(1)}, u32[]{:S(2)}, u32[]{:S(2)}) %collective-permute-start.33) | collective-permute-done | bytes 262176 | tf_op jit(solution)/shard_map/ppermute | solution.py:27
  179.7 4.1 %collective-permute-done.36 = bf16[128,1024]{1,0:T(8,128)(2,1)S(1)} collective-permute-done((bf16[128,1024]{1,0:T(8,128)(2,1)S(1)}, bf16[128,1024]{1,0:T(8,128)(2,1)S(1)}, u32[]{:S(2)}, u32[]{:S(2)}) %collective-permute-start.36) | collective-permute-done | bytes 262176 | tf_op jit(solution)/shard_map/ppermute | solution.py:27
  189.4 3.0 %collective-permute-done.37 = bf16[256,256]{1,0:T(8,128)(2,1)S(1)} collective-permute-done((bf16[256,256]{1,0:T(8,128)(2,1)S(1)}, bf16[256,256]{1,0:T(8,128)(2,1)S(1)}, u32[]{:S(2)}, u32[]{:S(2)}) %collective-permute-start.37) | collective-permute-done | bytes 131104 | tf_op jit(solution)/shard_map/ppermute | solution.py:571
  (119 shorter events, 62.8 us)
Async XLA Ops:
  1.9 16.8 %collective-permute-start.1 = (bf16[256,1024]{1,0:T(8,128)(2,1)S(1)}, bf16[256,1024]{1,0:T(8,128)(2,1)S(1)}, u32[]{:S(2)}, u32[]{:S(2)}) collective-permute-start(bf16[256,1024]{1,0:T(8,128)(2,1)S(1)} %constant_dynamic-slice_fusion.refs_3_.refs_4_), channel_id=1, source_target_pairs={{0,4},{1,5},{2,6},{3,7},{4,8},{5,9},{6,10},{7,11},{8,12},{9,13},{1... | collective-permute-start | bytes 1572872 | tf_op jit(solution)/shard_map/ppermute | solution.py:27
  8.5 11.2 %collective-permute-start.5 = (bf16[256,1024]{1,0:T(8,128)(2,1)S(1)}, bf16[256,1024]{1,0:T(8,128)(2,1)S(1)}, u32[]{:S(2)}, u32[]{:S(2)}) collective-permute-start(bf16[256,1024]{1,0:T(8,128)(2,1)S(1)} %constant_dynamic-slice_fusion.refs_3_.refs_4_), channel_id=1, source_target_pairs={{0,1},{1,2},{2,3},{3,0},{4,5},{5,6},{6,7},{7,4},{8,9},{9,10},{10,1... | collective-permute-start | bytes 1572872 | tf_op jit(solution)/shard_map/ppermute | solution.py:27
  10.5 14.8 %collective-permute-start.6 = (bf16[256,1024]{1,0:T(8,128)(2,1)S(1)}, bf16[256,1024]{1,0:T(8,128)(2,1)}, u32[]{:S(2)}, u32[]{:S(2)}) collective-permute-start(bf16[256,1024]{1,0:T(8,128)(2,1)S(1)} %constant_dynamic-slice_fusion.refs_3_.refs_4_), channel_id=1, source_target_pairs={{0,3},{1,0},{2,1},{3,2},{4,7},{5,4},{6,5},{7,6},{8,11},{9,8},{10,9... | collective-permute-start | bytes 1572872 | tf_op jit(solution)/shard_map/ppermute | solution.py:27
  12.6 12.7 %collective-permute-start = (bf16[256,1024]{1,0:T(8,128)(2,1)S(1)}, bf16[256,1024]{1,0:T(8,128)(2,1)}, u32[]{:S(2)}, u32[]{:S(2)}) collective-permute-start(bf16[256,1024]{1,0:T(8,128)(2,1)S(1)} %constant_dynamic-slice_fusion.refs_3_.refs_4_), channel_id=1, source_target_pairs={{0,12},{1,13},{2,14},{3,15},{4,0},{5,1},{6,2},{7,3},{8,4},{9,5},{1... | collective-permute-start | bytes 1572872 | tf_op jit(solution)/shard_map/ppermute | solution.py:27
  14.2 43.0 %all-to-all-start = ((bf16[8,48,4096]{2,1,0:T(8,128)(2,1)}), bf16[8,48,4096]{2,1,0:T(8,128)(2,1)}, u32[]{:S(2)}, u32[]{:S(2)}) async-start(bf16[8,48,4096]{2,1,0:T(8,128)(2,1)} %bitcast.32), calls=%async_computation | async-start | bytes 6291456 | tf_op jit(solution)/shard_map/all_to_all | solution.py:604
  18.8 15.6 %collective-permute-start.2 = (bf16[256,1024]{1,0:T(8,128)(2,1)S(1)}, bf16[256,1024]{1,0:T(8,128)(2,1)S(1)}, u32[]{:S(2)}, u32[]{:S(2)}) collective-permute-start(bf16[256,1024]{1,0:T(8,128)(2,1)S(1)} %collective-permute-done.1.refs_4_.refs_5_), channel_id=1, source_target_pairs={{0,4},{1,5},{2,6},{3,7},{4,8},{5,9},{6,10},{7,11},{8,12},{9,13},{1... | collective-permute-start | bytes 1572872 | tf_op jit(solution)/shard_map/ppermute | solution.py:27
  19.2 15.1 %collective-permute-start.3 = (bf16[256,1024]{1,0:T(8,128)(2,1)S(1)}, bf16[256,1024]{1,0:T(8,128)(2,1)S(1)}, u32[]{:S(2)}, u32[]{:S(2)}) collective-permute-start(bf16[256,1024]{1,0:T(8,128)(2,1)S(1)} %collective-permute-done.1.refs_4_.refs_5_), channel_id=1, source_target_pairs={{0,1},{1,2},{2,3},{3,0},{4,5},{5,6},{6,7},{7,4},{8,9},{9,10},{10,1... | collective-permute-start | bytes 1572872 | tf_op jit(solution)/shard_map/ppermute | solution.py:27
  19.7 14.6 %collective-permute-start.4 = (bf16[256,1024]{1,0:T(8,128)(2,1)S(1)}, bf16[256,1024]{1,0:T(8,128)(2,1)}, u32[]{:S(2)}, u32[]{:S(2)}) collective-permute-start(bf16[256,1024]{1,0:T(8,128)(2,1)S(1)} %collective-permute-done.1.refs_4_.refs_5_), channel_id=1, source_target_pairs={{0,3},{1,0},{2,1},{3,2},{4,7},{5,4},{6,5},{7,6},{8,11},{9,8},{10,9... | collective-permute-start | bytes 1572872 | tf_op jit(solution)/shard_map/ppermute | solution.py:27
  25.3 11.4 %collective-permute-start.9 = (bf16[256,1024]{1,0:T(8,128)(2,1)S(1)}, bf16[256,1024]{1,0:T(8,128)(2,1)}, u32[]{:S(2)}, u32[]{:S(2)}) collective-permute-start(bf16[256,1024]{1,0:T(8,128)(2,1)S(1)} %constant_dynamic-slice_fusion.refs_3_.refs_4_), channel_id=1, source_target_pairs={{0,16},{16,0},{1,17},{17,1},{2,18},{18,2},{3,19},{19,3},{4,20},{20... | collective-permute-start | bytes 1572872 | tf_op jit(solution)/shard_map/ppermute | solution.py:31
  25.3 11.6 %collective-permute-start.10 = (bf16[256,1024]{1,0:T(8,128)(2,1)S(1)}, bf16[256,1024]{1,0:T(8,128)(2,1)S(1)}, u32[]{:S(2)}, u32[]{:S(2)}) collective-permute-start(bf16[256,1024]{1,0:T(8,128)(2,1)S(1)} %collective-permute-done.1.refs_4_.refs_5_), channel_id=1, source_target_pairs={{0,16},{16,0},{1,17},{17,1},{2,18},{18,2},{3,19},{19,3},{4,20},{20... | collective-permute-start | bytes 1572872 | tf_op jit(solution)/shard_map/ppermute | solution.py:31
  36.6 16.6 %collective-permute-start.7 = (bf16[512,1024]{1,0:T(8,128)(2,1)S(1)}, bf16[512,1024]{1,0:T(8,128)(2,1)S(1)}, u32[]{:S(2)}, u32[]{:S(2)}) collective-permute-start(bf16[512,1024]{1,0:T(8,128)(2,1)S(1)} %constant_dynamic-update-slice_fusion.refs_5_.refs_6_), channel_id=1, source_target_pairs={{0,1},{1,2},{2,3},{3,0},{4,5},{5,6},{6,7},{7,4},{8,9},{9,10},{10,1... | collective-permute-start | bytes 3145736 | tf_op jit(solution)/shard_map/ppermute | solution.py:27
  37.7 15.5 %collective-permute-start.8 = (bf16[512,1024]{1,0:T(8,128)(2,1)S(1)}, bf16[512,1024]{1,0:T(8,128)(2,1)S(1)}, u32[]{:S(2)}, u32[]{:S(2)}) collective-permute-start(bf16[512,1024]{1,0:T(8,128)(2,1)S(1)} %constant_dynamic-update-slice_fusion.refs_5_.refs_6_), channel_id=1, source_target_pairs={{0,3},{1,0},{2,1},{3,2},{4,7},{5,4},{6,5},{7,6},{8,11},{9,8},{10,9... | collective-permute-start | bytes 3145736 | tf_op jit(solution)/shard_map/ppermute | solution.py:27
  53.8 18.6 %collective-permute-start.15 = (bf16[512,1024]{1,0:T(8,128)(2,1)}, bf16[512,1024]{1,0:T(8,128)(2,1)}, u32[]{:S(2)}, u32[]{:S(2)}) collective-permute-start(bf16[512,1024]{1,0:T(8,128)(2,1)} %constant_dynamic-update-slice_fusion.2.refs_6_.refs_7_), channel_id=1, source_target_pairs={{0,1},{1,2},{2,3},{3,0},{4,5},{5,6},{6,7},{7,4},{8,9},{9,10},{10,1... | collective-permute-start | bytes 3145736 | tf_op jit(solution)/shard_map/ppermute | solution.py:27
  54.9 17.5 %collective-permute-start.16 = (bf16[512,1024]{1,0:T(8,128)(2,1)S(1)}, bf16[512,1024]{1,0:T(8,128)(2,1)}, u32[]{:S(2)}, u32[]{:S(2)}) collective-permute-start(bf16[512,1024]{1,0:T(8,128)(2,1)S(1)} %collective-permute-done.8.refs_11_), channel_id=1, source_target_pairs={{0,3},{1,0},{2,1},{3,2},{4,7},{5,4},{6,5},{7,6},{8,11},{9,8},{10,9... | collective-permute-start | bytes 3145736 | tf_op jit(solution)/shard_map/ppermute | solution.py:27
  89.9 15.2 %collective-permute-start.21 = (bf16[192,4096]{1,0:T(8,128)(2,1)}, bf16[192,4096]{1,0:T(8,128)(2,1)}, u32[]{:S(2)}, u32[]{:S(2)}) collective-permute-start(bf16[192,4096]{1,0:T(8,128)(2,1)} %refs_0_), channel_id=1, source_target_pairs={{0,16},{16,0},{1,17},{17,1},{2,18},{18,2},{3,19},{19,3},{4,20},{20... | collective-permute-start | bytes 4718600 | tf_op jit(solution)/shard_map/ppermute | solution.py:31
  90.1 15.0 %collective-permute-start.22 = (bf16[192,4096]{1,0:T(8,128)(2,1)}, bf16[192,4096]{1,0:T(8,128)(2,1)}, u32[]{:S(2)}, u32[]{:S(2)}) collective-permute-start(bf16[192,4096]{1,0:T(8,128)(2,1)} %refs_1_.6), channel_id=1, source_target_pairs={{0,16},{16,0},{1,17},{17,1},{2,18},{18,2},{3,19},{19,3},{4,20},{20... | collective-permute-start | bytes 4718600 | tf_op jit(solution)/shard_map/ppermute | solution.py:31
  90.5 26.0 %all-to-all-start.1 = ((bf16[8,48,2048]{2,1,0:T(8,128)(2,1)}), bf16[8,48,2048]{2,1,0:T(8,128)(2,1)S(1)}, u32[]{:S(2)}, u32[]{:S(2)}) async-start(bf16[8,48,2048]{2,1,0:T(8,128)(2,1)} %bitcast.68), calls=%async_computation.1 | async-start | bytes 3145728 | tf_op jit(solution)/shard_map/all_to_all | solution.py:639
  124.0 16.1 %collective-permute-start.25 = (bf16[512,1024]{1,0:T(8,128)(2,1)S(1)}, bf16[512,1024]{1,0:T(8,128)(2,1)S(1)}, u32[]{:S(2)}, u32[]{:S(2)}) collective-permute-start(bf16[512,1024]{1,0:T(8,128)(2,1)S(1)} %get-tuple-element.113), channel_id=1, source_target_pairs={{0,4},{1,5},{2,6},{3,7},{4,8},{5,9},{6,10},{7,11},{8,12},{9,13},{1... | collective-permute-start | bytes 3145736 | tf_op jit(solution)/shard_map/ppermute | solution.py:27
  124.3 15.7 %collective-permute-start.26 = (bf16[512,1024]{1,0:T(8,128)(2,1)S(1)}, bf16[512,1024]{1,0:T(8,128)(2,1)S(1)}, u32[]{:S(2)}, u32[]{:S(2)}) collective-permute-start(bf16[512,1024]{1,0:T(8,128)(2,1)S(1)} %get-tuple-element.114), channel_id=1, source_target_pairs={{0,12},{1,13},{2,14},{3,15},{4,0},{5,1},{6,2},{7,3},{8,4},{9,5},{1... | collective-permute-start | bytes 3145736 | tf_op jit(solution)/shard_map/ppermute | solution.py:27
  129.8 21.0 %collective-permute-start.29 = (bf16[512,1024]{1,0:T(8,128)(2,1)S(1)}, bf16[512,1024]{1,0:T(8,128)(2,1)S(1)}, u32[]{:S(2)}, u32[]{:S(2)}) collective-permute-start(bf16[512,1024]{1,0:T(8,128)(2,1)S(1)} %get-tuple-element.123), channel_id=1, source_target_pairs={{0,12},{1,13},{2,14},{3,15},{4,0},{5,1},{6,2},{7,3},{8,4},{9,5},{1... | collective-permute-start | bytes 3145736 | tf_op jit(solution)/shard_map/ppermute | solution.py:27
  131.0 20.3 %collective-permute-start.30 = (bf16[512,1024]{1,0:T(8,128)(2,1)S(1)}, bf16[512,1024]{1,0:T(8,128)(2,1)S(1)}, u32[]{:S(2)}, u32[]{:S(2)}) collective-permute-start(bf16[512,1024]{1,0:T(8,128)(2,1)S(1)} %get-tuple-element.124), channel_id=1, source_target_pairs={{0,4},{1,5},{2,6},{3,7},{4,8},{5,9},{6,10},{7,11},{8,12},{9,13},{1... | collective-permute-start | bytes 3145736 | tf_op jit(solution)/shard_map/ppermute | solution.py:27
  142.9 19.6 %collective-permute-start.27 = (bf16[512,1024]{1,0:T(8,128)(2,1)S(1)}, bf16[512,1024]{1,0:T(8,128)(2,1)S(1)}, u32[]{:S(2)}, u32[]{:S(2)}) collective-permute-start(bf16[512,1024]{1,0:T(8,128)(2,1)S(1)} %get-tuple-element.121), channel_id=1, source_target_pairs={{0,4},{1,5},{2,6},{3,7},{4,8},{5,9},{6,10},{7,11},{8,12},{9,13},{1... | collective-permute-start | bytes 3145736 | tf_op jit(solution)/shard_map/ppermute | solution.py:27
  143.7 18.8 %collective-permute-start.28 = (bf16[512,1024]{1,0:T(8,128)(2,1)S(1)}, bf16[512,1024]{1,0:T(8,128)(2,1)S(1)}, u32[]{:S(2)}, u32[]{:S(2)}) collective-permute-start(bf16[512,1024]{1,0:T(8,128)(2,1)S(1)} %get-tuple-element.122), channel_id=1, source_target_pairs={{0,12},{1,13},{2,14},{3,15},{4,0},{5,1},{6,2},{7,3},{8,4},{9,5},{1... | collective-permute-start | bytes 3145736 | tf_op jit(solution)/shard_map/ppermute | solution.py:27
  166.4 7.7 %collective-permute-start.31 = (bf16[128,1024]{1,0:T(8,128)(2,1)S(1)}, bf16[128,1024]{1,0:T(8,128)(2,1)S(1)}, u32[]{:S(2)}, u32[]{:S(2)}) collective-permute-start(bf16[128,1024]{1,0:T(8,128)(2,1)S(1)} %get-tuple-element.153), channel_id=1, source_target_pairs={{0,1},{1,2},{2,3},{3,0},{4,5},{5,6},{6,7},{7,4},{8,9},{9,10},{10,1... | collective-permute-start | bytes 786440 | tf_op jit(solution)/shard_map/ppermute | solution.py:27
  (26 other events, 171.8 us)
